TPU v7x, 512 devices: a whole 4x8x8 slice. The times are simulated.
512 devices in a mesh: expert: 2 (over core), branch: 2 (over x_hi), seq: 16 (over z, x_lo), tensor: 8 (over y).
Axes of the slice: x: 4 (x_hi: 2, x_lo: 2; x = x_hi * 2 + x_lo), y: 8, z: 8, core: 2. Of those that a mesh axis runs over, the one named last changes fastest.
Arguments:
- query_raw: bfloat16 [2, 2, 2816, 5120], P('expert', 'branch', 'seq', 'tensor'), may hold values from -40 to 40
- key_raw: bfloat16 [2, 2, 2816, 5120], P('expert', 'branch', 'seq', 'tensor'), may hold values from -40 to 40
- value_rows: bfloat16 [2, 2, 2816, 5120], P('expert', 'branch', 'seq', 'tensor'), may hold values from -6 to 6
- residual: bfloat16 [2, 2, 2816, 5120], P('expert', 'branch', 'seq', 'tensor'), may hold values from -0.8 to 0.8
- latent: float32 [2, 2816, 64], P('expert', 'seq'), may hold values from -6 to 6
- query_gain: float32 [2, 5120], P('expert', 'tensor'), may hold values from 0.7 to 2.8
- key_gain: float32 [2, 5120], P('expert', 'tensor'), may hold values from 0.7 to 2.8
- out_weight: bfloat16 [2, 5120, 5120], P('expert', 'tensor', ('branch', 'seq')), may hold values from -0.078125 to 0.078125
- attn_gate: float32 [2, 5120], P('expert', 'tensor'), may hold values from -2 to 2
- head_shift: float32 [2, 5120], P('expert', 'tensor'), may hold values from -3 to 3
- head_scale: float32 [2, 5120], P('expert', 'tensor'), may hold values from -3 to 3
- head_weight: bfloat16 [2, 5120, 64], P('expert', 'tensor'), may hold values from -0.078125 to 0.078125
- head_bias: float32 [2, 64], P('expert'), may hold values from -3 to 3
- valid_rows: int32 [2], P('expert'), may hold values from 27 to 54
- step_index: int32 [2], P('expert'), may hold values from 0 to 39
Outputs:
- hidden_out: bfloat16 [2, 2, 2816, 5120], P('expert', 'branch', 'seq', 'tensor')
- velocity: float32 [2, 2816, 64], P('expert', 'seq')
- relayed: float32 [2, 2816, 64], P('expert', 'seq')
All inputs are finite; a program needn't handle non-finite values.
Results may differ from a plain program's by a relative error of at most 0.011.
The roundings to bfloat16 on the way count: a program that leaves them out, or rounds other values in their place, can miss the bound.
Values may be sent and summed in bfloat16 or wider, within the bound.
A program may use at most 64 MiB of HBM per device.

v0:
```python
import math

import jax
import jax.numpy as jnp
from jax import lax
from jax.sharding import PartitionSpec as P

D = 5120
HD = 128
GRID_H = 30
GRID_W = 52
STEPS = 40


EPSILON = 1e-06
THETA = 10000.0
FLOW_SHIFT = 12.0
GUIDE_HIGH = 4.0
GUIDE_LOW = 3.0
MASKED = -1e30


def from_partner(block, axis, stride):
    count = lax.axis_size(axis)
    route = []
    for low in range(count):
        high = low | 1 << stride
        if high != low and high < count:
            route += [(low, high), (high, low)]
    return lax.ppermute(block, axis, route)


def rope_tables(positions):
    half_pairs = HD // 2
    third_pairs = half_pairs // 3
    first_pairs = half_pairs - 2 * third_pairs
    frame_tokens = GRID_H * GRID_W
    frame_idx = (positions // frame_tokens).astype(jnp.float32)
    row_idx = (positions % frame_tokens // GRID_W).astype(jnp.float32)
    col_idx = (positions % GRID_W).astype(jnp.float32)
    pair_idx = jnp.arange(half_pairs, dtype=jnp.int32)
    in_time = pair_idx < first_pairs
    in_rows = pair_idx < first_pairs + third_pairs
    log_theta = math.log(THETA)
    rate_time = jnp.exp(-log_theta * pair_idx.astype(jnp.float32) / first_pairs)
    rate_rows = jnp.exp(-log_theta * (pair_idx - first_pairs).astype(jnp.float32) / third_pairs)
    rate_cols = jnp.exp(
        -log_theta * (pair_idx - first_pairs - third_pairs).astype(jnp.float32) / third_pairs
    )
    rates = jnp.where(in_time, rate_time, jnp.where(in_rows, rate_rows, rate_cols))
    coords = jnp.where(
        in_time[None, :],
        frame_idx[:, None],
        jnp.where(in_rows[None, :], row_idx[:, None], col_idx[:, None]),
    )
    angles = coords * rates[None, :]
    return (jnp.cos(angles), jnp.sin(angles))


def rotate(values, cosines, sines):
    rows = values.shape[0]
    heads_here = values.shape[1] // HD
    paired = values.reshape(rows, heads_here, HD // 2, 2)
    real_part = paired[..., 0]
    imag_part = paired[..., 1]
    cos_b = cosines[:, None, :]
    sin_b = sines[:, None, :]
    turned = jnp.stack(
        [real_part * cos_b - imag_part * sin_b, real_part * sin_b + imag_part * cos_b], axis=-1
    )
    return turned.reshape(rows, heads_here * HD)


def normalize_rotate(values, gain, squares, cosines, sines):
    inverse = lax.rsqrt(squares / D + EPSILON)
    return rotate(values * inverse[:, None] * gain[None, :], cosines, sines).astype(jnp.bfloat16)


def attend_block(carry, query_heads, key_block, value_block, key_start, key_limit):
    rows = key_block.shape[0]
    heads_here = query_heads.shape[1]
    key_heads = key_block.reshape(rows, heads_here, HD)
    value_heads = value_block.reshape(rows, heads_here, HD)
    logits = jnp.einsum(
        "qhd,khd->hqk", query_heads, key_heads, preferred_element_type=jnp.float32
    ) * HD ** (-0.5)
    key_live = key_start + jnp.arange(rows, dtype=jnp.int32) < key_limit
    logits = jnp.where(key_live[None, None, :], logits, MASKED)
    running_max, running_sum, accumulated = carry
    new_max = jnp.maximum(running_max, jnp.max(logits, axis=2))
    weights = jnp.where(key_live[None, None, :], jnp.exp(logits - new_max[:, :, None]), 0.0)
    shrink = jnp.exp(running_max - new_max)
    running_sum = running_sum * shrink + jnp.sum(weights, axis=2)
    mixed = jnp.einsum(
        "hqk,khd->qhd",
        weights.astype(jnp.bfloat16),
        value_heads,
        preferred_element_type=jnp.float32,
    )
    accumulated = accumulated * shrink.T[:, :, None] + mixed
    return (new_max, running_sum, accumulated)


def noise_level(frac):
    return FLOW_SHIFT * frac / (1.0 + (FLOW_SHIFT - 1.0) * frac)


def local(
    query_raw,
    key_raw,
    value_rows,
    residual,
    latent,
    query_gain,
    key_gain,
    out_weight,
    attn_gate,
    head_shift,
    head_scale,
    head_weight,
    head_bias,
    valid_rows,
    step_index,
):
    expert_id = lax.axis_index("expert")
    branch_id = lax.axis_index("branch")
    seq_id = lax.axis_index("seq")
    queries = query_raw[0, 0].astype(jnp.float32)
    keys_here = key_raw[0, 0].astype(jnp.float32)
    tokens_here, local_width = queries.shape
    heads_here = local_width // HD
    query_sq, key_sq = lax.psum(
        (jnp.sum(queries * queries, axis=1), jnp.sum(keys_here * keys_here, axis=1)), "tensor"
    )
    positions = seq_id * tokens_here + jnp.arange(tokens_here, dtype=jnp.int32)
    cosines, sines = rope_tables(positions)
    query_rot = normalize_rotate(queries, query_gain[0], query_sq, cosines, sines)
    key_rot = normalize_rotate(keys_here, key_gain[0], key_sq, cosines, sines)
    query_heads = query_rot.reshape(tokens_here, heads_here, HD)
    key_limit = valid_rows[0] * GRID_W
    initial = (
        jnp.full((heads_here, tokens_here), MASKED, jnp.float32),
        jnp.zeros((heads_here, tokens_here), jnp.float32),
        jnp.zeros((tokens_here, heads_here, HD), jnp.float32),
    )
    key_piece = lax.all_gather(key_rot, "seq", axis=0, tiled=True)
    value_piece = lax.all_gather(value_rows[0, 0], "seq", axis=0, tiled=True)
    rows = key_piece.shape[0]
    block = rows
    while block > 512 and block % 2 == 0:
        block = block // 2
    count = rows // block

    def one_block(turn, state):
        key_block = lax.dynamic_slice_in_dim(key_piece, turn * block, block, 0)
        value_block = lax.dynamic_slice_in_dim(value_piece, turn * block, block, 0)
        return attend_block(state, query_heads, key_block, value_block, turn * block, key_limit)

    running_max, running_sum, accumulated = lax.fori_loop(0, count, one_block, initial)
    attended = (
        (accumulated / running_sum.T[:, :, None])
        .reshape(tokens_here, local_width)
        .astype(jnp.bfloat16)
    )
    projected = jnp.dot(
        attended,
        lax.all_gather(out_weight[0], ("branch", "seq"), axis=1, tiled=True),
        preferred_element_type=jnp.float32,
    )
    mixed_cols = lax.psum_scatter(projected, "tensor", scatter_dimension=1, tiled=True)
    hidden_state = (residual[0, 0].astype(jnp.float32) + attn_gate[0][None, :] * mixed_cols).astype(
        jnp.bfloat16
    )
    hidden_f = hidden_state.astype(jnp.float32)
    scale_row = 1.0 + head_scale[0]
    shift_row = head_shift[0]
    weight_f = head_weight[0].astype(jnp.float32)
    bias_row = head_bias[0]
    guide = jnp.where(expert_id == 0, GUIDE_HIGH, GUIDE_LOW)
    branch_factor = jnp.where(branch_id == 0, guide, 1.0 - guide)
    row_sum, row_squares = lax.psum(
        (jnp.sum(hidden_f, axis=1), jnp.sum(hidden_f * hidden_f, axis=1)), "tensor"
    )
    row_mean = row_sum / D
    inv_std = lax.rsqrt(row_squares / D - row_mean * row_mean + EPSILON)
    head_in = (hidden_f - row_mean[:, None]) * inv_std[:, None] * scale_row[None, :] + shift_row[
        None, :
    ]
    partial_value = jnp.dot(head_in, weight_f, precision=lax.Precision.HIGHEST)
    branch_value = lax.psum(partial_value, "tensor") + bias_row[None, :]
    guided = lax.psum(branch_factor * branch_value, "branch")
    step_now = step_index[0].astype(jnp.float32)
    delta = noise_level(1.0 - (step_now + 1.0) / STEPS) - noise_level(1.0 - step_now / STEPS)
    advanced = latent[0] + delta * guided
    relayed = from_partner(advanced, "expert", 0)
    return (hidden_state[None, None], guided[None], relayed[None])


def solution(mesh):
    placed = (
        P("expert", "branch", "seq", "tensor"),
        P("expert", "branch", "seq", "tensor"),
        P("expert", "branch", "seq", "tensor"),
        P("expert", "branch", "seq", "tensor"),
        P("expert", "seq", None),
        P("expert", "tensor"),
        P("expert", "tensor"),
        P("expert", "tensor", ("branch", "seq")),
        P("expert", "tensor"),
        P("expert", "tensor"),
        P("expert", "tensor"),
        P("expert", "tensor", None),
        P("expert", None),
        P("expert"),
        P("expert"),
    )
    return jax.shard_map(
        local,
        mesh=mesh,
        in_specs=placed,
        out_specs=(
            P("expert", "branch", "seq", "tensor"),
            P("expert", "seq", None),
            P("expert", "seq", None),
        ),
        check_vma=False,
    )
```

profile of v0, /device:TPU:1, one launch (start us, length us, event | category | flops | bytes accessed | tf_op | source)
XLA Modules:
  0.0 506.9 jit_solution(14993881550748243954)
XLA Ops:
  7.3 1.1 multiply_reduce_fusion
  8.4 1.1 copy.32
  9.5 1.1 multiply_reduce_fusion.1
  11.9 14.7 %all-reduce.1 = (f32[176]{0:T(256)S(1)}, f32[176]{0:T(256)S(1)}) all-reduce(f32[176]{0:T(256)S(1)} %multiply_reduce_fusion.1, f32[176]{0:T(256)S(1)} %multiply_reduce_fusion), channel_id=1, replica_groups=mesh['expert'=2,'branch'=2,'seq'=16,'tensor'=8] {'tensor'}, use_global_device_ids=true, to_apply=%region_1.0 | all-reduce | flops 352 | bytes 2816 | tf_op jit(solution)/shard_map/psum | solution.py:132
  27.8 1.7 subtract_convert_fusion
  35.1 93.0 %all-gather.6.cloned.1.call-done = bf16[2816,640]{1,0:T(8,128)(2,1)} async-done(((bf16[176,640]{1,0:T(8,128)(2,1)}), bf16[2816,640]{1,0:T(8,128)(2,1)}) %all-gather.6.cloned.1.call-update) | async-done | bytes 3604496 | tf_op jit(solution)/shard_map/all_gather | solution.py:146
  128.2 93.1 %all-gather.8.cloned.1.call-done = bf16[1,1,2816,640]{3,2,1,0:T(8,128)(2,1)} async-done(((bf16[1,1,176,640]{3,2,1,0:T(8,128)(2,1)}), bf16[1,1,2816,640]{3,2,1,0:T(8,128)(2,1)}) %all-gather.8.cloned.1.call-update) | async-done | bytes 3604496 | tf_op jit(solution)/shard_map/all_gather | solution.py:147
  221.3 27.7 %while.18 = (s32[]{:T(128)}, f32[5,176]{1,0:T(8,128)S(1)}, f32[5,176]{1,0:T(8,128)S(1)}, f32[176,5,128]{2,0,1:T(8,128)S(1)}, s32[]{:T(128)}, /*index=5*/bf16[281...) while((s32[]{:T(128)}, f32[5,176]{1,0:T(8,128)S(1)}, ...), condition=%wide.region_7.8_spmd.clone, body=%wide.region_4.7_spmd.clone.sunk | while | flops 161728864 | bytes 9407035 | solution.py:159
  221.3 1.2 constant_dynamic-slice_fusion.3
  224.7 1.2 constant_dynamic-slice_fusion.3
  228.2 1.2 constant_dynamic-slice_fusion.3
  231.7 1.2 constant_dynamic-slice_fusion.3
  235.1 1.2 constant_dynamic-slice_fusion.3
  238.6 1.2 constant_dynamic-slice_fusion.3
  242.1 1.2 constant_dynamic-slice_fusion.3
  245.6 1.3 constant_dynamic-slice_fusion.3
  249.0 127.5 %all-gather.10.cloned.1.call-done = bf16[1,640,5120]{1,2,0:T(8,128)(2,1)} async-done(((bf16[1,640,160]{1,2,0:T(8,128)(2,1)}), bf16[1,640,5120]{1,2,0:T(8,128)(2,1)}) %all-gather.10.cloned.1.call-update) | async-done | bytes 6553616 | tf_op jit(solution)/shard_map/all_gather | solution.py:167
  376.5 7.0 %fusion.12 = f32[176,5120]{1,0:T(8,128)} fusion(bf16[1,640,5120]{1,2,0:T(8,128)(2,1)} %all-gather.10.cloned.1.call-done, f32[176,5,128]{2,0,1:T(8,128)S(1)} %get-tuple-element.143, f32[176,5]{0,1:T(8,128)S(1)} %bitcast.69), kind=kOutput, calls=%fused_computation.21 | convolution fusion | flops 1153658880 | bytes 10612160 | tf_op jit(solution)/shard_map/dot_general | solution.py:165
  384.6 54.2 %reduce-scatter.2.cloned.1.call-done = f32[176,640]{1,0:T(8,128)} async-done(((f32[176,5120]{1,0:T(8,128)}), f32[176,640]{1,0:T(8,128)}) %reduce-scatter.2.cloned.1.call-update) | async-done | bytes 450576 | tf_op jit(solution)/shard_map/reduce_scatter | solution.py:170
  438.8 1.2 convert_reduce_fusion
  440.0 11.9 %all-reduce = (f32[176]{0:T(256)S(1)}, f32[176]{0:T(256)S(1)}) all-reduce(f32[176]{0:T(256)S(1)} %get-tuple-element.189, f32[176]{0:T(256)S(1)} %get-tuple-element.188), channel_id=1, replica_groups=mesh['expert'=2,'branch'=2,'seq'=16,'tensor'=8] {'tensor'}, use_global_device_ids=true, to_apply=%region_12.13 | all-reduce | flops 352 | bytes 2816 | tf_op jit(solution)/shard_map/psum | solution.py:181
  452.5 20.6 %psum.46 = f32[176,64]{0,1:T(8,128)S(1)} all-reduce(f32[176,64]{0,1:T(8,128)S(1)} %fusion.17), channel_id=1, replica_groups=mesh['expert'=2,'branch'=2,'seq'=16,'tensor'=8] {'tensor'}, use_global_device_ids=true, to_apply=%region_13.14 | all-reduce | flops 11264 | bytes 90112 | tf_op jit(solution)/shard_map/psum | solution.py:190
  473.2 9.8 %psum.47 = f32[176,64]{0,1:T(8,128)S(1)} all-reduce(f32[176,64]{0,1:T(8,128)S(1)} %add_multiply_fusion), channel_id=1, replica_groups=mesh['expert'=2,'branch'=2,'seq'=16,'tensor'=8] {'branch'}, use_global_device_ids=true, to_apply=%region_14.15 | all-reduce | flops 11264 | bytes 90112 | tf_op jit(solution)/shard_map/psum | solution.py:191
  483.1 15.7 %collective-permute-start = (f32[176,64]{0,1:T(8,128)S(1)}, f32[176,64]{0,1:T(8,128)S(1)}, u32[]{:S(2)}, u32[]{:S(2)}) collective-permute-start(f32[176,64]{0,1:T(8,128)S(1)} %bitcast_add_fusion), channel_id=1, source_target_pairs={{0,256},{256,0},{1,257},{257,1},{2,258},{258,2},{3,259},{259,3},{4... | collective-permute-start | bytes 135176 | tf_op jit(solution)/shard_map/ppermute | solution.py:30
  (137 shorter events, 27.0 us)
Async XLA Ops:
  7.2 444.8 %copy-start = (bf16[1,640,64]{1,2,0:T(8,128)(2,1)S(1)}, bf16[1,640,64]{1,2,0:T(8,128)(2,1)}, u32[]{:S(2)}) copy-start(bf16[1,640,64]{1,2,0:T(8,128)(2,1)} %param.28) | copy-start | bytes 245764
  7.2 3.4 copy-start.1
  7.2 121.0 %all-gather.6.cloned.1.call-start = ((), (), s32[]{:S(2)}) async-start(), calls=%async_computation.1 | async-start | bytes 3829760 | tf_op jit(solution)/shard_map/all_gather | solution.py:146
  9.5 1.7 copy-start.6
  10.8 1.0 copy-start.7
  31.6 189.7 %all-gather.8.cloned.1.call-start = ((), (), s32[]{:S(2)}) async-start(), calls=%async_computation.3 | async-start | bytes 3829760 | tf_op jit(solution)/shard_map/all_gather | solution.py:147
  32.3 344.2 %all-gather.10.cloned.1.call-start = ((), (), s32[]{:S(2)}) async-start(), calls=%async_computation.4 | async-start | bytes 6758400 | tf_op jit(solution)/shard_map/all_gather | solution.py:167
  33.0 405.7 %reduce-scatter.2.cloned.1.call-start = ((), (), s32[]{:S(2)}) async-start(), calls=%async_computation.2 | async-start | bytes 4055040 | tf_op jit(solution)/shard_map/reduce_scatter | solution.py:170
  383.6 0.8 copy-start.8
  383.6 0.8 copy-start.9
  383.6 1.0 copy-start.10
  383.6 55.2 %copy-start.3 = (bf16[1,1,176,640]{3,2,1,0:T(8,128)(2,1)S(1)}, bf16[1,1,176,640]{3,2,1,0:T(8,128)(2,1)}, u32[]{:S(2)}) copy-start(bf16[1,1,176,640]{3,2,1,0:T(8,128)(2,1)} %param.20) | copy-start | bytes 675844
  383.6 89.5 %copy-start.11 = (f32[1,64]{1,0:T(1,128)S(1)}, f32[1,64]{1,0:T(1,128)}, u32[]{:S(2)}) copy-start(f32[1,64]{1,0:T(1,128)} %param.29) | copy-start | bytes 772
  383.6 99.4 %copy-start.5 = (f32[1,176,64]{1,2,0:T(8,128)S(1)}, f32[1,176,64]{1,2,0:T(8,128)}, u32[]{:S(2)}) copy-start(f32[1,176,64]{1,2,0:T(8,128)} %param.21) | copy-start | bytes 135172
  440.0 60.3 %copy-start.4 = (bf16[176,640]{1,0:T(8,128)(2,1)}, bf16[176,640]{1,0:T(8,128)(2,1)S(1)}, u32[]{:S(2)}) copy-start(bf16[176,640]{1,0:T(8,128)(2,1)S(1)} %get-tuple-element.212) | copy-start | bytes 675844
  483.0 17.3 %copy-start.2 = (f32[176,64]{0,1:T(8,128)}, f32[176,64]{0,1:T(8,128)S(1)}, u32[]{:S(2)}) copy-start(f32[176,64]{0,1:T(8,128)S(1)} %psum.47) | copy-start | bytes 135172
  483.1 16.6 %collective-permute-start = (f32[176,64]{0,1:T(8,128)S(1)}, f32[176,64]{0,1:T(8,128)S(1)}, u32[]{:S(2)}, u32[]{:S(2)}) collective-permute-start(f32[176,64]{0,1:T(8,128)S(1)} %bitcast_add_fusion), channel_id=1, source_target_pairs={{0,256},{256,0},{1,257},{257,1},{2,258},{258,2},{3,259},{259,3},{4... | collective-permute-start | bytes 135176 | tf_op jit(solution)/shard_map/ppermute | solution.py:30
Sparse Core Ops, SparseCore 0:
  31.7 96.4 all-gather.5
  130.2 90.9 all-gather.7
  223.4 153.1 all-gather.9
  383.7 54.9 reduce-scatter.1
where the time goes:
time: 507 us
  waiting for transfers between devices  370 us (73%)
  blocking collectives  57 us (11%)
  local copies, waits for them, and re-layouts  19 us (4%)
  matrix products  16 us (3%)
  starting transfers between devices  15.9 us (3%)
  between operations  15.7 us (3%)
  other arithmetic  12.7 us (3%)
    all_gather x1, waiting for transfers between devices, local(): lax.all_gather(out_weight[0], ('branch', 'seq'), axis=1, tiled=True)  127 us
    all_gather x1, waiting for transfers between devices, local(): value_piece = lax.all_gather(value_rows[0, 0], 'seq', axis=0, tiled=True)  93.1 us
    all_gather x1, waiting for transfers between devices, local(): key_piece = lax.all_gather(key_rot, 'seq', axis=0, tiled=True)  93 us
    reduce_scatter x1, waiting for transfers between devices, local(): lax.psum_scatter(projected, 'tensor', scatter_dimension=1, tiled=True)  54.2 us
    psum x1, blocking collectives, local(): branch_value = lax.psum(partial_value, 'tensor') + bias_row[None, :]  20.6 us
    ppermute x1, starting transfers between devices, from_partner(): return lax.ppermute(block, axis, route)  15.7 us
    psum x1, blocking collectives, local(): lax.psum((jnp.sum(queries * queries, axis=1), jnp.sum(keys_here * keys_he...  14.7 us
    dynamic_slice x16, local copies, waits for them, and re-layouts, one_block(): value_block = lax.dynamic_slice_in_dim(value_piece, turn * block, block, 0)  12.1 us
  transfers between devices with their start and end apart: 5, of which 5 were waited for; matrix products, arithmetic and copies ran while one was open for 6% of the time, Pallas kernels for 0%

commit v1 on v0

v1 whole, which is shorter than its diff:
```python
import math

import jax
import jax.numpy as jnp
from jax import lax
from jax.experimental import pallas as pl
from jax.experimental.pallas import tpu as pltpu
from jax.sharding import PartitionSpec as P

D = 5120
HD = 128
GRID_H = 30
GRID_W = 52
STEPS = 40
TOKENS = 2816
EPSILON = 1e-06
THETA = 10000.0
FLOW_SHIFT = 12.0
GUIDE_HIGH = 4.0
GUIDE_LOW = 3.0
MASKED = -1e30

ROWS = 176
WIDTH = 640
COLS = 160
LOCAL_HEADS = 5
HEAD_Z = (0, 1, 3, 4, 6)
SPLIT = 96
PIECE = 24
PADDED = 8 * PIECE
LIVE_FROM = 1280
MESH = pl.DeviceIdType.MESH
LOG2E = 1.4426950408889634


def add_mod(value, step, size):
    return lax.rem(value + (step % size), size)


def rope_tables(positions):
    half_pairs = HD // 2
    third_pairs = half_pairs // 3
    first_pairs = half_pairs - 2 * third_pairs
    frame_tokens = GRID_H * GRID_W
    frame_idx = (positions // frame_tokens).astype(jnp.float32)
    row_idx = (positions % frame_tokens // GRID_W).astype(jnp.float32)
    col_idx = (positions % GRID_W).astype(jnp.float32)
    lane = jnp.arange(HD, dtype=jnp.int32)
    pair_idx = lane // 2
    in_time = pair_idx < first_pairs
    in_rows = pair_idx < first_pairs + third_pairs
    log_theta = math.log(THETA)
    rate_time = jnp.exp(-log_theta * pair_idx.astype(jnp.float32) / first_pairs)
    rate_rows = jnp.exp(-log_theta * (pair_idx - first_pairs).astype(jnp.float32) / third_pairs)
    rate_cols = jnp.exp(
        -log_theta * (pair_idx - first_pairs - third_pairs).astype(jnp.float32) / third_pairs
    )
    rates = jnp.where(in_time, rate_time, jnp.where(in_rows, rate_rows, rate_cols))
    coords = jnp.where(
        in_time[None, :],
        frame_idx[:, None],
        jnp.where(in_rows[None, :], row_idx[:, None], col_idx[:, None]),
    )
    angles = coords * rates[None, :]
    sign = jnp.where(lane % 2 == 0, -1.0, 1.0)
    return (jnp.cos(angles), jnp.sin(angles) * sign[None, :])


def noise_level(frac):
    return FLOW_SHIFT * frac / (1.0 + (FLOW_SHIFT - 1.0) * frac)


def kernel(
    q_ref, k_ref, v_ref, res_ref, qg_ref, kg_ref, cos_ref, sin_ref, w_ref, gate_ref, scale_ref,
    shift_ref, hw_ref, bias_ref, mask_ref, lat_ref,
    hid_ref, vel_ref, rel_ref,
    sq_pad, msg, msg_in, qr, kr, keys, values, queries, logits, outs, att, wg, pk, pk_in,
    quad, fin, lat_in,
    msg_ss, msg_rs, v_ss, v_rs, k_ss, k_rs, q_ss, q_rs, o_ss, o_rs, ag_ss, ag_rs, wp_ss, wp_rs,
    wz_ss, wz_rs, wx_ss, wx_rs, wf_ss, wf_rs, pk_ss, pk_rs, qd_ss, qd_rs, fa_ss, fa_rs, lt_ss, lt_rs,
):
    e = lax.axis_index("expert")
    b = lax.axis_index("branch")
    s = lax.axis_index("seq")
    y = lax.axis_index("tensor")
    z = lax.div(s, 2)
    x_lo = lax.rem(s, 2)
    x = 2 * b + x_lo

    def remote(src, dst, send_sem, recv_sem, device):
        return pltpu.make_async_remote_copy(
            src_ref=src, dst_ref=dst, send_sem=send_sem, recv_sem=recv_sem,
            device_id=device, device_id_type=MESH,
        )

    def arrived(ref, sem):
        pltpu.make_async_copy(ref, ref, sem).wait()

    def x_device(where):
        return {"branch": lax.div(where, 2), "seq": 2 * z + lax.rem(where, 2)}

    def z_device(where):
        return {"seq": 2 * where + x_lo}

    x_up, x_down = add_mod(x, 1, 4), add_mod(x, -1, 4)
    z_up, z_down = add_mod(z, 1, 8), add_mod(z, -1, 8)
    y_up, y_down = add_mod(y, 1, 8), add_mod(y, -1, 8)

    w_to = {"branch": lax.rem(z, 2), "seq": 2 * y + x_lo, "tensor": 4 * b + lax.div(z, 2)}
    w_from = {
        "branch": lax.div(y, 4),
        "seq": 2 * (2 * lax.rem(y, 4) + b) + x_lo,
        "tensor": z,
    }
    w_stays = jnp.logical_and(
        jnp.logical_and(lax.rem(z, 2) == b, y == z), 4 * b + lax.div(z, 2) == y
    )

    barrier = pltpu.get_barrier_semaphore()

    def greet(device):
        pl.semaphore_signal(barrier, inc=1, device_id=device, device_id_type=MESH)

    for step in range(1, 16):
        greet({"seq": add_mod(s, step, 16)})
    for step in range(1, 8):
        greet({"tensor": add_mod(y, step, 8)})
    greet(x_device(x_up))
    greet(x_device(x_down))
    greet({"branch": 1 - b})
    greet({"expert": 1 - e})
    greet({"expert": 1 - e, "branch": 1 - b})

    @pl.when(jnp.logical_not(w_stays))
    def _():
        greet(w_from)

    def squares(ref):
        total = jnp.zeros((ROWS, HD), jnp.float32)
        for h in range(LOCAL_HEADS):
            part = ref[:, h * HD:(h + 1) * HD].astype(jnp.float32)
            total = total + part * part
        sq_pad[0:ROWS, :] = total
        return jnp.sum(sq_pad[...].T, axis=0, keepdims=True)

    sq_pad[ROWS:, :] = jnp.zeros((256 - ROWS, HD), jnp.float32)
    msg[...] = jnp.zeros_like(msg)
    msg[0:1, :] = squares(q_ref)
    msg[1:2, :] = squares(k_ref)
    weight_f = hw_ref[...].astype(jnp.float32)
    scale_row = 1.0 + scale_ref[...]
    msg[2:3, 0:64] = jnp.dot(scale_row, weight_f, precision=lax.Precision.HIGHEST)
    msg[3:4, 0:64] = jnp.dot(shift_ref[...], weight_f, precision=lax.Precision.HIGHEST)
    pk[ROWS:, :] = jnp.zeros((PADDED - ROWS, HD), jnp.float32)

    pl.semaphore_wait(barrier, 28 - w_stays.astype(jnp.int32))

    msg_copies = [
        remote(msg, msg_in.at[i - 1], msg_ss.at[i - 1], msg_rs.at[i - 1],
               {"tensor": add_mod(y, i, 8)})
        for i in range(1, 8)
    ]
    for copy in msg_copies:
        copy.start()

    my_rows = pl.ds(pl.multiple_of(s * ROWS, 16), ROWS)

    def to_head(src_of, dst, ss, rs):
        copies = []
        for h in range(LOCAL_HEADS):
            for half in range(2):
                target = 2 * HEAD_Z[h] + half
                src, place = src_of(h), dst.at[my_rows, :]
                copies.append((
                    s == target,
                    pltpu.make_async_copy(src, place, rs.at[s]),
                    remote(src, place, ss.at[2 * h + half], rs.at[s], {"seq": target}),
                ))
        return copies

    def start_all(copies):
        for here, local, far in copies:
            pl.when(here)(local.start)
            pl.when(jnp.logical_not(here))(far.start)

    def sent_all(copies):
        for here, local, far in copies:
            pl.when(jnp.logical_not(here))(far.wait_send)

    v_copies = to_head(lambda h: v_ref.at[:, pl.ds(h * HD, HD)], values, v_ss, v_rs)
    k_copies = to_head(lambda h: kr.at[h], keys, k_ss, k_rs)
    q_copies = []
    for h in range(LOCAL_HEADS):
        place = queries.at[z]
        q_copies.append((
            z == HEAD_Z[h],
            pltpu.make_async_copy(qr.at[h], place, q_rs.at[z]),
            remote(qr.at[h], place, q_ss.at[h], q_rs.at[z], z_device(HEAD_Z[h])),
        ))

    start_all(v_copies)
    lat_copy = remote(lat_ref, lat_in, lt_ss, lt_rs, {"expert": 1 - e})
    lat_copy.start()

    def w_slot(at_z, at_x, first=0, count=COLS):
        return wg.at[at_z, pl.ds(pl.multiple_of(at_x * COLS + first, 16), count), :]

    w_place = w_slot(y, 2 * lax.rem(z, 2) + x_lo)
    w_far = remote(w_ref, w_place, wp_ss, wp_rs, w_to)
    w_near = pltpu.make_async_copy(w_ref, w_place, wp_rs)
    pl.when(w_stays)(w_near.start)
    pl.when(jnp.logical_not(w_stays))(w_far.start)

    for i in range(7):
        arrived(msg_in.at[i], msg_rs.at[i])
    sums = msg[...]
    for i in range(7):
        sums = sums + msg_in[i]
    inverse = lax.rsqrt(sums[0:2, :] / D + EPSILON)
    head_u = sums[2:3, 0:64]
    head_c = sums[3:4, 0:64]

    even = lax.rem(lax.broadcasted_iota(jnp.int32, (ROWS, HD), 1), 2) == 0

    def normalize_rotate(ref, gain_ref, row, out):
        column = jnp.broadcast_to(inverse[row:row + 1, :], (HD, 256)).T[0:ROWS, :]
        for h in range(LOCAL_HEADS):
            part = ref[:, h * HD:(h + 1) * HD].astype(jnp.float32)
            part = part * column * gain_ref[:, h * HD:(h + 1) * HD]
            swapped = jnp.where(even, pltpu.roll(part, HD - 1, 1), pltpu.roll(part, 1, 1))
            out[h] = (part * cos_ref[...] + swapped * sin_ref[...]).astype(jnp.bfloat16)

    normalize_rotate(k_ref, kg_ref, 1, kr)
    start_all(k_copies)
    normalize_rotate(q_ref, qg_ref, 0, qr)
    start_all(q_copies)

    half_cols = COLS // 2
    wz_copies = []
    for step in range(1, 5):
        up_slot = add_mod(z, -(step - 1), 8)
        down_slot = add_mod(z, step - 1, 8)
        if step < 4:
            up, down = w_slot(up_slot, x), w_slot(down_slot, x)
        else:
            up = w_slot(up_slot, x, 0, half_cols)
            down = w_slot(down_slot, x, half_cols, half_cols)
        wz_copies.append((
            remote(up, up, wz_ss.at[0, step - 1], wz_rs.at[0, step - 1], z_device(z_up)),
            remote(down, down, wz_ss.at[1, step - 1], wz_rs.at[1, step - 1], z_device(z_down)),
        ))

    def z_slot(j):
        k = (j + 1) // 2
        return add_mod(z, k if j % 2 else -k, 8)

    wx_copies, wf_copies = [], []
    for j in range(8):
        at_z = z_slot(j)
        own = w_slot(at_z, x)
        wx_copies.append((
            remote(own, own, wx_ss.at[j, 0], wx_rs.at[j, 0], x_device(x_up)),
            remote(own, own, wx_ss.at[j, 1], wx_rs.at[j, 1], x_device(x_down)),
        ))
        first = w_slot(at_z, x_down, 0, half_cols)
        second = w_slot(at_z, x_up, half_cols, half_cols)
        wf_copies.append((
            remote(first, first, wf_ss.at[j, 0], wf_rs.at[j, 0], x_device(x_up)),
            remote(second, second, wf_ss.at[j, 1], wf_rs.at[j, 1], x_device(x_down)),
        ))

    def w_event(j):
        if j == 0:
            arrived(w_slot(z, x), wp_rs)
            wz_copies[0][0].start()
            wz_copies[0][1].start()
        elif j < 7:
            k = (j + 1) // 2
            way = j % 2
            arrived(w_slot(z_slot(j), x), wz_rs.at[way, k - 1])
            if k < 4:
                wz_copies[k][way].start()
        elif j == 7:
            arrived(w_slot(z_slot(7), x, 0, half_cols), wz_rs.at[0, 3])
            arrived(w_slot(z_slot(7), x, half_cols, half_cols), wz_rs.at[1, 3])
        if j < 8:
            wx_copies[j][0].start()
            wx_copies[j][1].start()
        if j > 0:
            at_z = z_slot(j - 1)
            arrived(w_slot(at_z, x_down), wx_rs.at[j - 1, 0])
            wf_copies[j - 1][0].start()
            arrived(w_slot(at_z, x_up), wx_rs.at[j - 1, 1])
            wf_copies[j - 1][1].start()

    w_event(0)
    w_event(1)
    w_event(2)

    attends = z == HEAD_Z[0]
    head = jnp.int32(0)
    for h in range(1, LOCAL_HEADS):
        attends = jnp.logical_or(attends, z == HEAD_Z[h])
        head = head + (z >= HEAD_Z[h]).astype(jnp.int32)
    head_cols = pl.ds(pl.multiple_of(head * HD, HD), HD)
    att_place = att.at[y, :, head_cols]

    @pl.when(attends)
    def _():
        for i in range(8):
            arrived(queries.at[i], q_rs.at[i])
        for i in range(16):
            arrived(keys.at[pl.ds(i * ROWS, ROWS), :], k_rs.at[i])
        for i in range(16):
            arrived(values.at[pl.ds(i * ROWS, ROWS), :], v_rs.at[i])

    def o_far(j):
        return remote(outs.at[j], att_place, o_ss.at[j], o_rs.at[head], z_device(j))

    factor = HD ** -0.5 * LOG2E

    def attend(j):
        query = queries[j]
        peak = None
        for c in range(TOKENS // 256):
            cols = slice(c * 256, (c + 1) * 256)
            part = lax.dot_general(
                query, keys[cols, :], (((1,), (1,)), ((), ())),
                preferred_element_type=jnp.float32,
            )
            if c * 256 >= LIVE_FROM:
                part = part + mask_ref[:, cols]
            logits[:, cols] = part
            top = jnp.maximum(part[:, 0:HD], part[:, HD:])
            peak = top if peak is None else jnp.maximum(peak, top)
        peak = jnp.max(peak, axis=1, keepdims=True)
        total = jnp.zeros((ROWS, HD), jnp.float32)
        mixed = jnp.zeros((ROWS, HD), jnp.float32)
        for c in range(TOKENS // 256):
            cols = slice(c * 256, (c + 1) * 256)
            prob = jnp.exp2((logits[:, cols] - peak) * factor)
            total = total + (prob[:, 0:HD] + prob[:, HD:])
            mixed = mixed + jnp.dot(
                prob.astype(jnp.bfloat16), values[cols, :], preferred_element_type=jnp.float32
            )
        denom = jnp.sum(total, axis=1, keepdims=True)
        outs[j] = (mixed / denom).astype(jnp.bfloat16)

    def one_block(j, carry):
        @pl.when(attends)
        def _():
            attend(j)
            pl.when(j == z)(
                pltpu.make_async_copy(outs.at[j], att_place, o_rs.at[head]).start
            )
            pl.when(j != z)(o_far(j).start)

        for turn, event in ((2, 3), (5, 4)):
            @pl.when(j == turn)
            def _():
                w_event(event)
        return carry

    lax.fori_loop(0, 8, one_block, 0)

    ag_copies = []
    for step in range(1, 5):
        up_block = att.at[add_mod(y, -(step - 1), 8)]
        down_block = att.at[add_mod(y, step - 1, 8)]
        if step == 4:
            up_block = up_block.at[pl.ds(0, SPLIT), :]
            down_block = down_block.at[pl.ds(SPLIT, ROWS - SPLIT), :]
        ag_copies.append((
            remote(up_block, up_block, ag_ss.at[0, step - 1], ag_rs.at[0, step - 1],
                   {"tensor": y_up}),
            remote(down_block, down_block, ag_ss.at[1, step - 1], ag_rs.at[1, step - 1],
                   {"tensor": y_down}),
        ))

    for h in range(LOCAL_HEADS):
        arrived(att.at[y, :, pl.ds(h * HD, HD)], o_rs.at[h])
    for step in range(1, 5):
        ag_copies[step - 1][0].start()
        ag_copies[step - 1][1].start()
        if step < 4:
            w_event(4 + step)
            arrived(att.at[add_mod(y, -step, 8)], ag_rs.at[0, step - 1])
            arrived(att.at[add_mod(y, step, 8)], ag_rs.at[1, step - 1])
    w_event(8)
    across = att.at[add_mod(y, 4, 8)]
    arrived(across.at[pl.ds(0, SPLIT), :], ag_rs.at[0, 3])
    arrived(across.at[pl.ds(SPLIT, ROWS - SPLIT), :], ag_rs.at[1, 3])
    for j in range(8):
        at_z = z_slot(j)
        arrived(w_slot(at_z, add_mod(x, 2, 4), 0, half_cols), wf_rs.at[j, 0])
        arrived(w_slot(at_z, add_mod(x, 2, 4), half_cols, half_cols), wf_rs.at[j, 1])

    projected = jnp.zeros((ROWS, WIDTH), jnp.float32)
    for t in range(8):
        projected = projected + lax.dot_general(
            att[t], wg[t], (((1,), (1,)), ((), ())), preferred_element_type=jnp.float32
        )
    hidden = (res_ref[...].astype(jnp.float32) + gate_ref[...] * projected).astype(jnp.bfloat16)
    hid_ref[...] = hidden
    hidden_f = hidden.astype(jnp.float32)
    pk[0:ROWS, 0:64] = jnp.dot(
        hidden_f * scale_row, weight_f, precision=lax.Precision.HIGHEST
    )
    lane = lax.broadcasted_iota(jnp.int32, (ROWS, 64), 1)
    row_sum = jnp.sum(hidden_f, axis=1, keepdims=True)
    row_sq = jnp.sum(hidden_f * hidden_f, axis=1, keepdims=True)
    pk[0:ROWS, 64:128] = jnp.where(lane == 0, row_sum, jnp.where(lane == 1, row_sq, 0.0))

    def piece(ref, at):
        return ref.at[pl.ds(pl.multiple_of(at * PIECE, 8), PIECE), :]

    pk_copies = [
        remote(piece(pk, add_mod(y, i, 8)), pk_in.at[i - 1], pk_ss.at[i - 1], pk_rs.at[i - 1],
               {"tensor": add_mod(y, i, 8)})
        for i in range(1, 8)
    ]
    for copy in pk_copies:
        copy.start()
    my_piece = pl.ds(pl.multiple_of(y * PIECE, 8), PIECE)
    total = pk[my_piece, :]
    for i in range(7):
        arrived(pk_in.at[i], pk_rs.at[i])
    for i in range(7):
        total = total + pk_in[i]
    mean = total[:, 64:65] / D
    inv_std = lax.rsqrt(total[:, 65:66] / D - mean * mean + EPSILON)
    value = inv_std * (total[:, 0:64] - mean * head_u) + head_c + bias_ref[...]
    slot = 2 * e + b
    quad[slot, :, 0:64] = value
    quad[slot, :, 64:128] = value
    qd_copies = [
        remote(quad.at[slot], quad.at[slot], qd_ss.at[i], qd_rs.at[i], device)
        for i, device in enumerate((
            {"branch": 1 - b}, {"expert": 1 - e}, {"expert": 1 - e, "branch": 1 - b},
        ))
    ]
    for copy in qd_copies:
        copy.start()
    arrived(lat_in, lt_rs)
    arrived(quad.at[2 * e + (1 - b)], qd_rs.at[0])
    arrived(quad.at[2 * (1 - e) + b], qd_rs.at[1])
    arrived(quad.at[2 * (1 - e) + (1 - b)], qd_rs.at[2])

    def guided(expert):
        guide = jnp.where(expert == 0, GUIDE_HIGH, GUIDE_LOW)
        cond, uncond = quad[2 * expert], quad[2 * expert + 1]
        return uncond + guide * (cond - uncond)

    latent = lat_in[my_piece, :]
    fin[my_piece, 0:64] = guided(e)[:, 0:64]
    fin[my_piece, 64:128] = latent[:, 0:64] + latent[:, 64:128] * guided(1 - e)[:, 0:64]
    fa_copies = [
        remote(piece(fin, y), piece(fin, y), fa_ss.at[i - 1], fa_rs.at[i - 1],
               {"tensor": add_mod(y, i, 8)})
        for i in range(1, 8)
    ]
    for copy in fa_copies:
        copy.start()
    for i in range(1, 8):
        arrived(piece(fin, add_mod(y, -i, 8)), fa_rs.at[i - 1])
    vel_ref[...] = fin[0:ROWS, 0:64]
    rel_ref[...] = fin[0:ROWS, 64:128]

    for copy in msg_copies + pk_copies + qd_copies + fa_copies + [lat_copy]:
        copy.wait_send()
    sent_all(v_copies + k_copies + q_copies)
    pl.when(jnp.logical_not(w_stays))(w_far.wait_send)
    for up, down in wz_copies + wx_copies + wf_copies + ag_copies:
        up.wait_send()
        down.wait_send()

    @pl.when(attends)
    def _():
        for j in range(8):
            pl.when(z != j)(o_far(j).wait_send)


def local(
    query_raw,
    key_raw,
    value_rows,
    residual,
    latent,
    query_gain,
    key_gain,
    out_weight,
    attn_gate,
    head_shift,
    head_scale,
    head_weight,
    head_bias,
    valid_rows,
    step_index,
):
    seq_id = lax.axis_index("seq")
    positions = seq_id * ROWS + jnp.arange(ROWS, dtype=jnp.int32)
    cosines, sines = rope_tables(positions)
    key_live = jnp.arange(TOKENS, dtype=jnp.int32) < valid_rows[0] * GRID_W
    mask = jnp.where(key_live, 0.0, MASKED)[None, :].astype(jnp.float32)
    step_now = step_index[0].astype(jnp.float32)
    delta = noise_level(1.0 - (step_now + 1.0) / STEPS) - noise_level(1.0 - step_now / STEPS)
    latent_delta = jnp.pad(
        jnp.concatenate([latent[0], jnp.broadcast_to(delta, latent[0].shape)], axis=1),
        ((0, PADDED - ROWS), (0, 0)),
    )
    vmem = pl.BlockSpec(memory_space=pltpu.VMEM)
    dma = pltpu.SemaphoreType.DMA
    f32, bf16 = jnp.float32, jnp.bfloat16
    hidden, velocity, relayed = pl.pallas_call(
        kernel,
        out_shape=(
            jax.ShapeDtypeStruct((ROWS, WIDTH), bf16),
            jax.ShapeDtypeStruct((ROWS, 64), f32),
            jax.ShapeDtypeStruct((ROWS, 64), f32),
        ),
        in_specs=[vmem] * 16,
        out_specs=(vmem, vmem, vmem),
        scratch_shapes=[
            pltpu.VMEM((256, HD), f32),
            pltpu.VMEM((8, 256), f32),
            pltpu.VMEM((7, 8, 256), f32),
            pltpu.VMEM((LOCAL_HEADS, ROWS, HD), bf16),
            pltpu.VMEM((LOCAL_HEADS, ROWS, HD), bf16),
            pltpu.VMEM((TOKENS, HD), bf16),
            pltpu.VMEM((TOKENS, HD), bf16),
            pltpu.VMEM((8, ROWS, HD), bf16),
            pltpu.VMEM((ROWS, TOKENS), f32),
            pltpu.VMEM((8, ROWS, HD), bf16),
            pltpu.VMEM((8, ROWS, WIDTH), bf16),
            pltpu.VMEM((8, WIDTH, WIDTH), bf16),
            pltpu.VMEM((PADDED, HD), f32),
            pltpu.VMEM((7, PIECE, HD), f32),
            pltpu.VMEM((4, PIECE, HD), f32),
            pltpu.VMEM((PADDED, HD), f32),
            pltpu.VMEM((PADDED, HD), f32),
            dma((7,)), dma((7,)),
            dma((10,)), dma((16,)),
            dma((10,)), dma((16,)),
            dma((5,)), dma((8,)),
            dma((8,)), dma((5,)),
            dma((2, 4)), dma((2, 4)),
            dma, dma,
            dma((2, 4)), dma((2, 4)),
            dma((8, 2)), dma((8, 2)),
            dma((8, 2)), dma((8, 2)),
            dma((7,)), dma((7,)),
            dma((3,)), dma((3,)),
            dma((7,)), dma((7,)),
            dma, dma,
        ],
        compiler_params=pltpu.CompilerParams(
            collective_id=0, has_side_effects=True, vmem_limit_bytes=56 * 1024 * 1024
        ),
    )(
        query_raw[0, 0], key_raw[0, 0], value_rows[0, 0], residual[0, 0], query_gain, key_gain,
        cosines, sines, out_weight[0].T, attn_gate, head_scale, head_shift, head_weight[0],
        head_bias, mask, latent_delta,
    )
    return (hidden[None, None], velocity[None], relayed[None])


def solution(mesh):
    placed = (
        P("expert", "branch", "seq", "tensor"),
        P("expert", "branch", "seq", "tensor"),
        P("expert", "branch", "seq", "tensor"),
        P("expert", "branch", "seq", "tensor"),
        P("expert", "seq", None),
        P("expert", "tensor"),
        P("expert", "tensor"),
        P("expert", "tensor", ("branch", "seq")),
        P("expert", "tensor"),
        P("expert", "tensor"),
        P("expert", "tensor"),
        P("expert", "tensor", None),
        P("expert", None),
        P("expert"),
        P("expert"),
    )
    return jax.shard_map(
        local,
        mesh=mesh,
        in_specs=placed,
        out_specs=(
            P("expert", "branch", "seq", "tensor"),
            P("expert", "seq", None),
            P("expert", "seq", None),
        ),
        check_vma=False,
    )
```

time: 507 us -> 156 us (0.31)
  waiting for transfers between devices: 370 us -> 0 us
  Pallas kernels: 0 us -> 146 us
  blocking collectives: 57 us -> 0 us
  matrix products: 16 us -> 0 us
  starting transfers between devices: 15.9 us -> 0 us
  local copies, waits for them, and re-layouts: 19 us -> 5.1 us
  between operations: 15.7 us -> 2.11 us
  other arithmetic: 12.7 us -> 2.45 us
    all_gather x3 -> x0, waiting for transfers between devices: 314 us -> none  [the longest x1 127 us: local(): lax.all_gather(out_weight[0], ('branch', 'seq'), axis=1, tiled=True)]
    pallas_call x0 -> x1, Pallas kernels: none -> 146 us  [local(): pl.pallas_call(kernel, out_shape=(jax.ShapeDtypeStruct((ROWS, WIDTH), bf1...]
    psum x4 -> x0, blocking collectives: 57 us -> none  [the longest x1 20.6 us: local(): branch_value = lax.psum(partial_value, 'tensor') + bias_row[None, :]]
    reduce_scatter x1 -> x0, waiting for transfers between devices: 54.2 us -> none  [local(): lax.psum_scatter(projected, 'tensor', scatter_dimension=1, tiled=True)]
    dot_general x18 -> x0, matrix products: 16 us -> none  [the longest x1 7.05 us: local(): jnp.dot(attended, lax.all_gather(out_weight[0], ('branch', 'seq'), axis=1...]
    ppermute x1 -> x0, starting transfers between devices: 15.7 us -> none  [from_partner(): return lax.ppermute(block, axis, route)]
    dynamic_slice x24 -> x0, local copies, waits for them, and re-layouts: 14.3 us -> none  [the longest x16 12.1 us: one_block(): value_block = lax.dynamic_slice_in_dim(value_piece, turn * block, block, 0)]
    reduce_sum x11 -> x0, other arithmetic: 7.67 us -> none  [the longest x8 4.34 us: attend_block(): running_sum = running_sum * shrink + jnp.sum(weights, axis=2)]
  transfers between devices with their start and end apart: 5 -> 0, of which waited for: 5 -> 0; matrix products, arithmetic and copies ran while one was open for 6% -> 0% of each run, Pallas kernels for 0% -> 0%
where the time goes in v1:
time: 156 us; the launch traced here: 155 us
  Pallas kernels  146 us (94%)
  local copies, waits for them, and re-layouts  5.1 us (3%)
  other arithmetic  2.45 us (2%)
  between operations  2.11 us (1%)
    pallas_call x1, Pallas kernels, local(): pl.pallas_call(kernel, out_shape=(jax.ShapeDtypeStruct((ROWS, WIDTH), bf1...  146 us
    unnamed x11, local copies, waits for them, and re-layouts  5.1 us

profile of v1, /device:TPU:1, one launch (start us, length us, event | category | flops | bytes accessed | tf_op | source)
XLA Modules:
  0.0 155.5 jit_solution(6124402580801087250)
XLA Ops:
  0.6 0.0 copy-start.2
  2.1 0.6 compare_select_fusion.mask_ref
  2.8 0.0 copy-done.2
  2.8 0.1 copy.19
  2.9 0.0 copy-start.1
  2.9 0.7 pad_select_fusion.lat_ref
  3.5 0.3 copy-done.1
  3.8 0.8 copy.18
  4.6 1.1 sine_multiply_fusion
  5.7 145.8 %shard_map.166 = (bf16[176,640]{1,0:T(8,128)(2,1)}, f32[176,64]{1,0:T(8,128)}, f32[176,64]{1,0:T(8,128)}) custom-call(bf16[176,640]{1,0:T(8,128)(2,1)} %bitcast.16, bf16[176,640]{1,0:T(8,128)(2,1)} %bitcast.17, bf16[176,640]{1,0:T(8,128)(2,1)} %bitcast.18, bf16[176,640]{1,0:T(8,128)(2,1)} %bitcast.19, f32[1,640]{1,0:T(1,128)} %qg_ref.1, f32[1,640]{1,0:T(1,128)} %kg_ref.1, ...), custom_call_target="tpu_custom_call" | custom-call | tf_op jit(solution)/shard_map/pallas_call | solution.py:514
  151.6 0.0 copy-start
  151.6 1.6 %copy.20 = f32[1,176,64]{1,2,0:T(8,128)} copy(f32[1,176,64]{2,1,0:T(8,128)} %bitcast.23) | data formatting | bytes 90112
  153.2 1.6 %copy.21 = f32[1,176,64]{1,2,0:T(8,128)} copy(f32[1,176,64]{2,1,0:T(8,128)} %bitcast.22) | data formatting | bytes 90112
  154.8 0.0 copy-done
  154.8 0.7 copy.25
  (4 shorter events, 0.1 us)
Async XLA Ops:
  0.6 2.1 %copy-start.2 = (f32[1,176,64]{1,2,0:T(8,128)S(1)}, f32[1,176,64]{1,2,0:T(8,128)}, u32[]{:S(2)}) copy-start(f32[1,176,64]{1,2,0:T(8,128)} %param.19) | copy-start | bytes 135172
  2.9 0.9 copy-start.1
  151.6 3.3 %copy-start = (bf16[176,640]{1,0:T(8,128)(2,1)S(1)}, bf16[176,640]{1,0:T(8,128)(2,1)}, u32[]{:S(2)}) copy-start(bf16[176,640]{1,0:T(8,128)(2,1)} %get-tuple-element.6) | copy-start | bytes 675844

commit v2 on v0

v2 whole, which is shorter than its diff:
```python
import math

import jax
import jax.numpy as jnp
from jax import lax
from jax.experimental import pallas as pl
from jax.experimental.pallas import tpu as pltpu
from jax.sharding import PartitionSpec as P

D = 5120
HD = 128
GRID_H = 30
GRID_W = 52
STEPS = 40
TOKENS = 2816
EPSILON = 1e-06
THETA = 10000.0
FLOW_SHIFT = 12.0
GUIDE_HIGH = 4.0
GUIDE_LOW = 3.0
MASKED = -1e30

ROWS = 176
WIDTH = 640
COLS = 160
LOCAL_HEADS = 5
HEAD_Z = (0, 1, 3, 4, 6)
UPPER = 96
W_COPIES = 31
LIVE_FROM = 1280
MESH = pl.DeviceIdType.MESH
LOG2E = 1.4426950408889634


def add_mod(value, step, size):
    return lax.rem(value + (step % size), size)


def rope_tables(first_position):
    half_pairs = HD // 2
    third_pairs = half_pairs // 3
    first_pairs = half_pairs - 2 * third_pairs
    frame_tokens = GRID_H * GRID_W
    position = first_position + lax.broadcasted_iota(jnp.int32, (ROWS, HD), 0)
    frame = (position >= frame_tokens).astype(jnp.int32)
    for later in range(2, (TOKENS - 1) // frame_tokens + 1):
        frame = frame + (position >= later * frame_tokens).astype(jnp.int32)
    inside = (position - frame * frame_tokens).astype(jnp.float32)
    row = jnp.floor((inside + 0.5) * (1.0 / GRID_W))
    col = inside - row * GRID_W
    lane = lax.broadcasted_iota(jnp.int32, (ROWS, HD), 1)
    pair = lax.shift_right_logical(lane, 1)
    in_time = pair < first_pairs
    in_rows = pair < first_pairs + third_pairs
    offset = jnp.where(in_time, 0, jnp.where(in_rows, first_pairs, first_pairs + third_pairs))
    count = jnp.where(in_time, float(first_pairs), float(third_pairs))
    rates = jnp.exp(-math.log(THETA) * (pair - offset).astype(jnp.float32) / count)
    coords = jnp.where(in_time, frame.astype(jnp.float32), jnp.where(in_rows, row, col))
    angles = coords * rates
    odd = jnp.bitwise_and(lane, 1) == 1
    sines = jnp.sin(angles)
    return jnp.cos(angles), jnp.where(odd, sines, -sines), odd


def noise_level(frac):
    return FLOW_SHIFT * frac / (1.0 + (FLOW_SHIFT - 1.0) * frac)


def kernel(
    q_ref, k_ref, v_ref, res_ref, qg_ref, kg_ref, w_ref, gate_ref, scale_ref,
    shift_ref, hw_ref, bias_ref, lat_ref, valid_ref, step_ref,
    hid_ref, vel_ref, rel_ref,
    sq_pad, msg, msg_in, cos, sin, qr, kr, keys, values, queries, mask, logits, outs, att, w_mid, wg, total, px, px_in,
    head_w, bias_row, lat, pk, pk_in, swap, swap_in, fin,
    msg_ss, msg_rs, v_ss, v_rs, k_ss, k_rs, q_ss, q_rs, vr_ss, vr_rs, kr_ss, kr_rs, o_ss, o_rs,
    ag_ss, ag_rs, wm_ss, wm_rs, wp_ss, wp_rs, w_ss, w_rs, px_ss, px_rs, pk_ss, pk_rs, sw_ss, sw_rs,
    fin_ss, fin_rs,
):
    e = lax.axis_index("expert")
    b = lax.axis_index("branch")
    s = lax.axis_index("seq")
    y = lax.axis_index("tensor")
    z = lax.div(s, 2)
    x_lo = lax.rem(s, 2)
    share = 2 * y + b

    def remote(src, dst, send_sem, recv_sem, device):
        return pltpu.make_async_remote_copy(
            src_ref=src, dst_ref=dst, send_sem=send_sem, recv_sem=recv_sem,
            device_id=device, device_id_type=MESH,
        )

    def arrived(ref, sem):
        pltpu.make_async_copy(ref, ref, sem).wait()

    def z_device(where):
        return {"seq": 2 * where + x_lo}

    def share_device(where):
        return {"branch": lax.rem(where, 2), "tensor": lax.div(where, 2)}

    z_up, z_down = add_mod(z, 1, 8), add_mod(z, -1, 8)
    y_up, y_down = add_mod(y, 1, 8), add_mod(y, -1, 8)
    beside = {"seq": s + 1 - 2 * x_lo}

    across = {"branch": 1 - b, "seq": 2 * z + 1 - x_lo}
    holds = lax.rem(y + b, 2) == 0
    off = lax.rem(y + b, 2)

    mid_z = 2 * lax.rem(lax.div(y, 2) + 4 - lax.div(z, 2), 4) + lax.rem(z, 2)
    to_y = 4 * b + lax.div(mid_z, 2)
    w_turns = lax.rem(y, 2) != b
    w_to = {
        "branch": lax.rem(y, 2),
        "seq": 2 * z + jnp.where(w_turns, 1 - x_lo, x_lo),
        "tensor": to_y,
    }
    turned = lax.div(y, 4) != b
    w_from = {
        "branch": lax.div(y, 4),
        "seq": 2 * z + jnp.where(turned, 1 - x_lo, x_lo),
        "tensor": 2 * lax.rem(lax.div(z, 2) + y, 4) + b,
    }
    w_stays_mid = mid_z == z
    w_stays = jnp.logical_and(lax.rem(y, 2) == b, to_y == y)

    barrier = pltpu.get_barrier_semaphore()

    def greet(device):
        pl.semaphore_signal(barrier, inc=1, device_id=device, device_id_type=MESH)

    for step in range(1, 8):
        greet(z_device(add_mod(z, step, 8)))
    for step in range(8):
        greet({"branch": 1 - b, "seq": 2 * add_mod(z, step, 8) + 1 - x_lo})
    for step in range(1, 16):
        greet(share_device(add_mod(share, step, 16)))
    greet(beside)
    greet({"expert": 1 - e})
    pl.when(jnp.logical_not(w_stays))(lambda: greet(w_from))

    def squares(ref):
        summed = jnp.zeros((ROWS, HD), jnp.float32)
        for h in range(LOCAL_HEADS):
            part = ref[:, h * HD:(h + 1) * HD].astype(jnp.float32)
            summed = summed + part * part
        sq_pad[0:ROWS, :] = summed
        return jnp.sum(sq_pad[...].T, axis=0, keepdims=True)

    sq_pad[ROWS:, :] = jnp.zeros((256 - ROWS, HD), jnp.float32)
    msg[...] = jnp.zeros_like(msg)
    for at, ref in enumerate((q_ref, k_ref)):
        row = squares(ref)
        msg[2 * at:2 * at + 1, :] = row[:, 0:HD]
        msg[2 * at + 1:2 * at + 2, :] = row[:, HD:]

    pl.semaphore_wait(barrier, 33 - w_stays.astype(jnp.int32))

    w_mid_far = remote(w_ref, w_mid, wm_ss, wm_rs, z_device(mid_z))
    w_mid_near = pltpu.make_async_copy(w_ref, w_mid, wm_rs)
    pl.when(w_stays_mid)(w_mid_near.start)
    pl.when(jnp.logical_not(w_stays_mid))(w_mid_far.start)

    msg_copies = [
        remote(msg, msg_in.at[i - 1], msg_ss.at[i - 1], msg_rs.at[i - 1],
               {"tensor": add_mod(y, i, 8)})
        for i in range(1, 8)
    ]
    for copy in msg_copies:
        copy.start()

    my_rows = pl.ds(pl.multiple_of(s * ROWS, 16), ROWS)

    def to_head(src_of, place, ss, rs):
        copies = []
        for h in range(LOCAL_HEADS):
            copies.append((
                z == HEAD_Z[h],
                pltpu.make_async_copy(src_of(h), place, rs.at[z]),
                remote(src_of(h), place, ss.at[h], rs.at[z], z_device(HEAD_Z[h])),
            ))
        return copies

    def start_all(copies):
        for here, local_copy, far in copies:
            pl.when(here)(local_copy.start)
            pl.when(jnp.logical_not(here))(far.start)

    def sent_all(copies):
        for here, _, far in copies:
            pl.when(jnp.logical_not(here))(far.wait_send)

    v_copies = to_head(lambda h: v_ref.at[:, pl.ds(h * HD, HD)], values.at[my_rows, :], v_ss, v_rs)
    k_copies = to_head(lambda h: kr.at[h], keys.at[my_rows, :], k_ss, k_rs)
    q_copies = to_head(lambda h: qr.at[h], queries.at[z], q_ss, q_rs)
    start_all(v_copies)

    cos_table, sin_table, odd = rope_tables(s * ROWS)
    cos[...] = cos_table
    sin[...] = sin_table
    limit = valid_ref[0] * GRID_W
    key_at = lax.broadcasted_iota(jnp.int32, (1, TOKENS), 1)
    mask[...] = jnp.where(key_at < limit, 0.0, MASKED)
    bias_row[...] = jnp.zeros_like(bias_row)
    bias_row[:, 0:64] = bias_ref[...]
    bias_col = jnp.broadcast_to(bias_row[...], (HD, HD)).T[0:64, 0:1]
    weight_f = hw_ref[...].astype(jnp.float32)
    scaled = weight_f * (1.0 + scale_ref[...])
    head_u = jnp.sum(scaled, axis=1, keepdims=True)
    head_c = jnp.sum(weight_f * shift_ref[...], axis=1, keepdims=True)
    head_c = head_c + jnp.where(y == 0, bias_col, 0.0)
    lane = lax.broadcasted_iota(jnp.int32, (64, HD), 1)
    extra = jnp.where(lane == ROWS - HD, head_u, jnp.where(lane == ROWS - HD + 1, head_c, 0.0))
    head_w[...] = jnp.zeros_like(head_w)
    pk[...] = jnp.zeros_like(pk)
    swap[...] = jnp.zeros_like(swap)
    fin[...] = jnp.zeros_like(fin)
    for i in range(16):
        head_w[8 * i:8 * i + 4, :] = scaled[4 * i:4 * i + 4, :]
        head_w[8 * i + 4:8 * i + 5, :] = jnp.ones((1, WIDTH), jnp.float32)
        pk[i, 0:4, HD:] = extra[4 * i:4 * i + 4, :]
        lat[i, 0:4, :] = lat_ref[4 * i:4 * i + 4, :]

    for i in range(7):
        arrived(msg_in.at[i], msg_rs.at[i])
    sums = msg[...]
    for i in range(7):
        sums = sums + msg_in[i]
    inverse = lax.rsqrt(sums / D + EPSILON)

    def normalize_rotate(ref, gain_ref, first, out):
        column = jnp.concatenate(
            [
                jnp.broadcast_to(inverse[first:first + 1, :], (HD, HD)).T,
                jnp.broadcast_to(inverse[first + 1:first + 2, :], (HD, HD)).T[0:ROWS - HD, :],
            ],
            axis=0,
        )
        for h in range(LOCAL_HEADS):
            part = ref[:, h * HD:(h + 1) * HD].astype(jnp.float32)
            part = part * column * gain_ref[:, h * HD:(h + 1) * HD]
            swapped = jnp.where(odd, pltpu.roll(part, 1, 1), pltpu.roll(part, HD - 1, 1))
            out[h] = (part * cos[...] + swapped * sin[...]).astype(jnp.bfloat16)

    normalize_rotate(k_ref, kg_ref, 2, kr)
    start_all(k_copies)
    normalize_rotate(q_ref, qg_ref, 0, qr)
    start_all(q_copies)

    slots = {}
    base_x = jnp.where(turned, 1 - x_lo, x_lo)
    for dz in range(8):
        at_z = add_mod(z, dz, 8)
        at = lax.rem(lax.div(at_z, 2) + y, 4)
        for dx in range(2):
            at_x = 1 - base_x if dx else base_x
            slots[dz, dx] = (at, (2 * lax.rem(at_z, 2) + at_x) * COLS)

    def w_slot(dz, dx, first=0, count=COLS):
        at, row = slots[dz % 8, dx]
        return wg.at[at, pl.ds(pl.multiple_of(row + first, 16), count), :]

    def upper(dz, dx):
        return w_slot(dz, dx, 0, UPPER)

    def lower(dz, dx):
        return w_slot(dz, dx, UPPER, COLS - UPPER)

    def upper_half(dz, way):
        return w_slot(dz, 0, way * (UPPER // 2), UPPER // 2)

    w_sent, w_index = {}, {}

    def w_copy(key, block, device):
        at = w_index.setdefault(key, len(w_index))
        w_sent[key] = remote(block, block, w_ss.at[at], w_rs.at[at], device)

    def w_wait(key, block):
        arrived(block, w_rs.at[w_index[key]])

    z_to = (z_device(z_up), z_device(z_down))

    def ring_slot(j):
        k = (j + 1) // 2
        return k if j % 2 else -k

    for way in range(2):
        sign = 1 if way else -1
        for k in range(1, 5):
            held = sign * (k - 1)
            w_copy(("z", k, way), upper(held, 0) if k < 4 else upper_half(held, way), z_to[way])
            for dx in range(2):
                if k < 4 or dx == way:
                    w_copy(("lz", k, way, dx), lower(held, dx), z_to[way])
    w_copy("lx", lower(0, 0), beside)
    for j in range(8):
        w_copy(("ux", j), upper(ring_slot(j), 0), beside)

    w_near = pltpu.make_async_copy(w_mid, w_slot(0, 0), wp_rs)
    to_row = (2 * lax.rem(z, 2) + x_lo) * COLS
    w_far = remote(
        w_mid, wg.at[lax.div(y, 2), pl.ds(pl.multiple_of(to_row, 16), COLS), :], wp_ss, wp_rs,
        w_to,
    )

    def w_event(name):
        if name == "along y":
            arrived(w_mid, wm_rs)
            pl.when(w_stays)(w_near.start)
            pl.when(jnp.logical_not(w_stays))(w_far.start)
        elif name == "start":
            arrived(w_slot(0, 0), wp_rs)
            w_sent["lx"].start()
            for way in range(2):
                w_sent["z", 1, way].start()
            for way in range(2):
                w_sent["lz", 1, way, 0].start()
            w_sent["ux", 0].start()
        elif name == "lower":
            w_wait("lx", lower(0, 1))
            for way in range(2):
                w_sent["lz", 1, way, 1].start()
        elif name == "end":
            for way in range(2):
                w_wait(("z", 4, way), upper_half(4, way))
            w_sent["ux", 7].start()
        elif name == "finish":
            for dx in range(2):
                w_wait(("lz", 4, dx, dx), lower(4, dx))
            for j in range(8):
                w_wait(("ux", j), upper(ring_slot(j), 1))
        else:
            k = name
            for way in (1, 0):
                held = k if way else -k
                w_wait(("z", k, way), upper(held, 0))
                w_sent["z", k + 1, way].start()
                w_sent["ux", 2 * k - way].start()
            for dx in range(2):
                for way in (1, 0):
                    w_wait(("lz", k, way, dx), lower(k if way else -k, dx))
                    if k < 3 or dx == way:
                        w_sent["lz", k + 1, way, dx].start()

    attends = z == HEAD_Z[0]
    head = jnp.int32(0)
    for h in range(1, LOCAL_HEADS):
        attends = jnp.logical_or(attends, z == HEAD_Z[h])
        head = head + (z >= HEAD_Z[h]).astype(jnp.int32)
    head_cols = pl.ds(pl.multiple_of(head * HD, HD), HD)
    att_place = att.at[lax.div(y, 2), b, :, head_cols]

    def block_rows(buf, at_z, at_x):
        return buf.at[pl.ds(pl.multiple_of((2 * at_z + at_x) * ROWS, 16), ROWS), :]

    def relay(buf, at_z, ss, rs):
        block = block_rows(buf, at_z, x_lo)
        return remote(block, block, ss.at[at_z], rs.at[at_z], beside)

    def pass_on(buf, came, ss, rs):
        @pl.when(attends)
        def _():
            def one(i, carry):
                arrived(block_rows(buf, i, x_lo), came.at[i])
                relay(buf, i, ss, rs).start()
                return carry

            lax.fori_loop(0, 8, one, 0)

    pass_on(values, v_rs, vr_ss, vr_rs)
    w_event('along y')
    pass_on(keys, k_rs, kr_ss, kr_rs)

    @pl.when(attends)
    def _():
        def one(i, carry):
            arrived(queries.at[i], q_rs.at[i])
            arrived(block_rows(keys, i, 1 - x_lo), kr_rs.at[i])
            arrived(block_rows(values, i, 1 - x_lo), vr_rs.at[i])
            return carry

        lax.fori_loop(0, 8, one, 0)

    def o_far(at_z):
        return remote(
            outs.at[at_z], att_place, o_ss.at[at_z], o_rs.at[b, head],
            {"branch": lax.rem(y, 2), "seq": 2 * at_z + jnp.where(holds, x_lo, 1 - x_lo)},
        )

    factor = HD ** -0.5 * LOG2E

    def attend(at_z):
        query = queries[at_z]
        peak = None
        for c in range(TOKENS // 256):
            cols = slice(c * 256, (c + 1) * 256)
            part = lax.dot_general(
                query, keys[cols, :], (((1,), (1,)), ((), ())),
                preferred_element_type=jnp.float32,
            )
            if c * 256 >= LIVE_FROM:
                part = part + mask[:, cols]
            logits[:, cols] = part
            top = jnp.maximum(part[:, 0:HD], part[:, HD:])
            peak = top if peak is None else jnp.maximum(peak, top)
        peak = jnp.max(peak, axis=1, keepdims=True)
        summed = jnp.zeros((ROWS, HD), jnp.float32)
        mixed = jnp.zeros((ROWS, HD), jnp.float32)
        for c in range(TOKENS // 256):
            cols = slice(c * 256, (c + 1) * 256)
            prob = jnp.exp2((logits[:, cols] - peak) * factor)
            summed = summed + (prob[:, 0:HD] + prob[:, HD:])
            mixed = mixed + jnp.dot(
                prob.astype(jnp.bfloat16), values[cols, :], preferred_element_type=jnp.float32
            )
        denom = jnp.sum(summed, axis=1, keepdims=True)
        outs[at_z] = (mixed / denom).astype(jnp.bfloat16)

    def one_block(j, carry):
        away = lax.div(8 - j, 2)
        at_z = lax.rem(z + jnp.where(lax.rem(j, 2) == 1, away, 8 - away), 8)

        @pl.when(attends)
        def _():
            attend(at_z)
            stays = jnp.logical_and(at_z == z, holds)
            pl.when(stays)(pltpu.make_async_copy(outs.at[at_z], att_place, o_rs.at[b, head]).start)
            pl.when(jnp.logical_not(stays))(o_far(at_z).start)

        for turn, event in ((0, 'start'), (2, 'lower'), (5, 1)):
            pl.when(j == turn)(lambda: w_event(event))
        return carry

    lax.fori_loop(0, 8, one_block, 0)

    def ag_block(way, away, token_branch, h):
        at_y = lax.rem(y + (away if way else 8 - away), 8)
        return att.at[lax.div(at_y, 2), token_branch, :, pl.ds(h * HD, HD)]

    def ag_last(way, h):
        return h >= 3 if way else h < 3

    ag_starts, ag_lasts = [], []
    for which in range(2):
        for h in range(LOCAL_HEADS):
            at = LOCAL_HEADS * which + h
            tb = b if which else 1 - b
            for way in range(2):
                device = {"tensor": y_down if way else y_up}
                near = ag_block(way, off, tb, h)
                ag_starts.append((which, h, way, remote(
                    near, near, ag_ss.at[way, 0, at], ag_rs.at[way, 0, at], device)))
                far = ag_block(way, off + 2, tb, h)
                ag_lasts.append((which, h, way, remote(
                    far, far, ag_ss.at[way, 1, at], ag_rs.at[way, 1, at], device)))

    def ag_start(which):
        for part, h, way, copy in ag_starts:
            if part != which:
                continue
            at = LOCAL_HEADS * which + h
            tb = b if which else 1 - b
            if way == 0:
                place = att.at[lax.div(y, 2), tb, :, pl.ds(h * HD, HD)]
                pl.when(holds)(lambda: arrived(place, o_rs.at[tb, h]))
            near = ag_block(way, off, tb, h)
            pl.when(jnp.logical_not(holds))(lambda: arrived(near, ag_rs.at[way, 0, at]))
            copy.start()

    def ag_go_on(which):
        for part, h, way, copy in ag_lasts:
            if part != which:
                continue
            at = LOCAL_HEADS * which + h
            arrived(ag_block(way, off + 2, b if which else 1 - b, h), ag_rs.at[way, off, at])
            if ag_last(way, h):
                copy.start()
            else:
                pl.when(holds)(copy.start)

    def ag_finish(which):
        @pl.when(holds)
        def _():
            for h in range(LOCAL_HEADS):
                way = 0 if ag_last(0, h) else 1
                opposite = ag_block(way, 4, b if which else 1 - b, h)
                arrived(opposite, ag_rs.at[way, 1, LOCAL_HEADS * which + h])

    def project(tb):
        def one_group(g, carry):
            part = lax.dot_general(
                att[g, tb], wg[g], (((1,), (1,)), ((), ())), preferred_element_type=jnp.float32
            )
            total[...] += part
            return carry

        total[...] = jnp.zeros_like(total)
        lax.fori_loop(0, 4, one_group, 0)
        return total[...]

    ag_start(0)
    w_event(2)
    ag_start(1)
    w_event(3)
    ag_go_on(0)
    w_event('end')
    ag_go_on(1)
    ag_finish(0)
    w_event('finish')
    px[...] = project(1 - b).astype(jnp.bfloat16)
    px_copy = remote(px, px_in, px_ss, px_rs, across)
    px_copy.start()
    ag_finish(1)
    projected = project(b)
    arrived(px_in, px_rs)
    projected = projected + px_in[...].astype(jnp.float32)
    hidden = (res_ref[...].astype(jnp.float32) + gate_ref[...] * projected).astype(jnp.bfloat16)
    hid_ref[...] = hidden
    hidden_f = hidden.astype(jnp.float32)

    over_features = (((1,), (1,)), ((), ()))
    sums = lax.dot_general(
        head_w[...], hidden_f, over_features, precision=lax.Precision.HIGHEST,
        preferred_element_type=jnp.float32,
    ).reshape(16, 8, ROWS)
    square_sums = lax.dot_general(
        jnp.ones((8, WIDTH), jnp.float32), hidden_f * hidden_f, over_features,
        precision=lax.Precision.HIGHEST, preferred_element_type=jnp.float32,
    )
    sixth = lax.broadcasted_iota(jnp.int32, (16, 8, ROWS), 1) == 5
    pk[:, :, 0:ROWS] = jnp.where(sixth, square_sums[None], sums)

    def share_copies(src_of, dst, ss, rs):
        return [
            remote(src_of(add_mod(share, r, 16)), dst.at[share], ss.at[r - 1], rs.at[r - 1],
                   share_device(add_mod(share, r, 16)))
            for r in range(1, 16)
        ]

    pk_copies = share_copies(lambda to: pk.at[to], pk_in, pk_ss, pk_rs)
    for copy in pk_copies:
        copy.start()
    pk_in[share] = pk[share]
    for r in range(1, 16):
        arrived(pk_in.at[add_mod(share, -r, 16)], pk_rs.at[r - 1])

    def branch_value(branch):
        got = pk_in[branch]
        for i in range(1, 8):
            got = got + pk_in[2 * i + branch]
        mean = got[4:5, 0:ROWS] / D
        inv_std = lax.rsqrt(got[5:6, 0:ROWS] / D - mean * mean + EPSILON)
        return (
            inv_std * (got[0:4, 0:ROWS] - mean * got[0:4, ROWS:ROWS + 1])
            + got[0:4, ROWS + 1:ROWS + 2]
        )

    cond, uncond = branch_value(0), branch_value(1)
    guide = jnp.where(e == 0, GUIDE_HIGH, GUIDE_LOW)
    guided = uncond + guide * (cond - uncond)
    step_now = jnp.full((4, ROWS), step_ref[0], jnp.int32).astype(jnp.float32)
    delta = noise_level(1.0 - (step_now + 1.0) / STEPS) - noise_level(1.0 - step_now / STEPS)
    swap[0:4, 0:ROWS] = lat[share][0:4, :] + delta * guided
    swap_copy = remote(swap, swap_in, sw_ss, sw_rs, {"expert": 1 - e})
    swap_copy.start()
    fin[share, 0:4, 0:ROWS] = guided
    arrived(swap_in, sw_rs)
    fin[share, 4:8, 0:ROWS] = swap_in[0:4, 0:ROWS]
    fin_copies = share_copies(lambda to: fin.at[share], fin, fin_ss, fin_rs)
    for copy in fin_copies:
        copy.start()
    for r in range(1, 16):
        arrived(fin.at[add_mod(share, -r, 16)], fin_rs.at[r - 1])
    for i in range(16):
        vel_ref[4 * i:4 * i + 4, :] = fin[i, 0:4, 0:ROWS]
        rel_ref[4 * i:4 * i + 4, :] = fin[i, 4:8, 0:ROWS]

    for copy in msg_copies + pk_copies + fin_copies + [swap_copy, px_copy]:
        copy.wait_send()
    sent_all(v_copies + k_copies + q_copies)
    pl.when(jnp.logical_not(w_stays_mid))(w_mid_far.wait_send)
    pl.when(jnp.logical_not(w_stays))(w_far.wait_send)
    for copy in w_sent.values():
        copy.wait_send()
    for _, _, _, copy in ag_starts:
        copy.wait_send()
    for _, h, way, copy in ag_lasts:
        if ag_last(way, h):
            copy.wait_send()
        else:
            pl.when(holds)(copy.wait_send)

    @pl.when(attends)
    def _():
        def one(i, carry):
            relay(values, i, vr_ss, vr_rs).wait_send()
            relay(keys, i, kr_ss, kr_rs).wait_send()
            pl.when(jnp.logical_not(jnp.logical_and(i == z, holds)))(o_far(i).wait_send)
            return carry

        lax.fori_loop(0, 8, one, 0)


def local(
    query_raw,
    key_raw,
    value_rows,
    residual,
    latent,
    query_gain,
    key_gain,
    out_weight,
    attn_gate,
    head_shift,
    head_scale,
    head_weight,
    head_bias,
    valid_rows,
    step_index,
):
    vmem = pl.BlockSpec(memory_space=pltpu.VMEM)
    smem = pl.BlockSpec(memory_space=pltpu.SMEM)
    dma = pltpu.SemaphoreType.DMA
    f32, bf16 = jnp.float32, jnp.bfloat16
    hidden, velocity, relayed = pl.pallas_call(
        kernel,
        out_shape=(
            jax.ShapeDtypeStruct((ROWS, WIDTH), bf16),
            jax.ShapeDtypeStruct((64, ROWS), f32),
            jax.ShapeDtypeStruct((64, ROWS), f32),
        ),
        in_specs=[vmem] * 13 + [smem] * 2,
        out_specs=(vmem, vmem, vmem),
        scratch_shapes=[
            pltpu.VMEM((256, HD), f32),
            pltpu.VMEM((8, HD), f32),
            pltpu.VMEM((7, 8, HD), f32),
            pltpu.VMEM((ROWS, HD), f32),
            pltpu.VMEM((ROWS, HD), f32),
            pltpu.VMEM((LOCAL_HEADS, ROWS, HD), bf16),
            pltpu.VMEM((LOCAL_HEADS, ROWS, HD), bf16),
            pltpu.VMEM((TOKENS, HD), bf16),
            pltpu.VMEM((TOKENS, HD), bf16),
            pltpu.VMEM((8, ROWS, HD), bf16),
            pltpu.VMEM((1, TOKENS), f32),
            pltpu.VMEM((ROWS, TOKENS), f32),
            pltpu.VMEM((8, ROWS, HD), bf16),
            pltpu.VMEM((4, 2, ROWS, WIDTH), bf16),
            pltpu.VMEM((COLS, WIDTH), bf16),
            pltpu.VMEM((4, WIDTH, WIDTH), bf16),
            pltpu.VMEM((ROWS, WIDTH), f32),
            pltpu.VMEM((ROWS, WIDTH), bf16),
            pltpu.VMEM((ROWS, WIDTH), bf16),
            pltpu.VMEM((128, WIDTH), f32),
            pltpu.VMEM((1, HD), f32),
            pltpu.VMEM((16, 4, ROWS), f32),
            pltpu.VMEM((16, 8, 256), f32),
            pltpu.VMEM((16, 8, 256), f32),
            pltpu.VMEM((8, 256), f32),
            pltpu.VMEM((8, 256), f32),
            pltpu.VMEM((16, 8, 256), f32),
            dma((7,)), dma((7,)),
            dma((5,)), dma((8,)),
            dma((5,)), dma((8,)),
            dma((5,)), dma((8,)),
            dma((8,)), dma((8,)),
            dma((8,)), dma((8,)),
            dma((8,)), dma((2, 5)),
            dma((2, 2, 10)), dma((2, 2, 10)),
            dma, dma,
            dma, dma,
            dma((W_COPIES,)), dma((W_COPIES,)),
            dma, dma,
            dma((15,)), dma((15,)),
            dma, dma,
            dma((15,)), dma((15,)),
        ],
        compiler_params=pltpu.CompilerParams(
            collective_id=0, has_side_effects=True, vmem_limit_bytes=56 * 1024 * 1024
        ),
    )(
        query_raw[0, 0], key_raw[0, 0], value_rows[0, 0], residual[0, 0], query_gain, key_gain,
        out_weight[0].T, attn_gate, head_scale, head_shift, head_weight[0].T, head_bias,
        latent[0].T, valid_rows, step_index,
    )
    return (hidden[None, None], velocity.T[None], relayed.T[None])


def solution(mesh):
    placed = (
        P("expert", "branch", "seq", "tensor"),
        P("expert", "branch", "seq", "tensor"),
        P("expert", "branch", "seq", "tensor"),
        P("expert", "branch", "seq", "tensor"),
        P("expert", "seq", None),
        P("expert", "tensor"),
        P("expert", "tensor"),
        P("expert", "tensor", ("branch", "seq")),
        P("expert", "tensor"),
        P("expert", "tensor"),
        P("expert", "tensor"),
        P("expert", "tensor", None),
        P("expert", None),
        P("expert"),
        P("expert"),
    )
    return jax.shard_map(
        local,
        mesh=mesh,
        in_specs=placed,
        out_specs=(
            P("expert", "branch", "seq", "tensor"),
            P("expert", "seq", None),
            P("expert", "seq", None),
        ),
        check_vma=False,
    )
```

time: 507 us -> 126 us (0.25)
  waiting for transfers between devices: 370 us -> 0 us
  Pallas kernels: 0 us -> 121 us
  blocking collectives: 57 us -> 0 us
  matrix products: 16 us -> 0 us
  starting transfers between devices: 15.9 us -> 0 us
  local copies, waits for them, and re-layouts: 19 us -> 3.17 us
  between operations: 15.7 us -> 1.95 us
  other arithmetic: 12.7 us -> 0 us
    all_gather x3 -> x0, waiting for transfers between devices: 314 us -> none  [the longest x1 127 us: local(): lax.all_gather(out_weight[0], ('branch', 'seq'), axis=1, tiled=True)]
    pallas_call x0 -> x1, Pallas kernels: none -> 121 us  [local(): pl.pallas_call(kernel, out_shape=(jax.ShapeDtypeStruct((ROWS, WIDTH), bf1...]
    psum x4 -> x0, blocking collectives: 57 us -> none  [the longest x1 20.6 us: local(): branch_value = lax.psum(partial_value, 'tensor') + bias_row[None, :]]
    reduce_scatter x1 -> x0, waiting for transfers between devices: 54.2 us -> none  [local(): lax.psum_scatter(projected, 'tensor', scatter_dimension=1, tiled=True)]
    dot_general x18 -> x0, matrix products: 16 us -> none  [the longest x1 7.05 us: local(): jnp.dot(attended, lax.all_gather(out_weight[0], ('branch', 'seq'), axis=1...]
    ppermute x1 -> x0, starting transfers between devices: 15.7 us -> none  [from_partner(): return lax.ppermute(block, axis, route)]
    dynamic_slice x24 -> x0, local copies, waits for them, and re-layouts: 14.3 us -> none  [the longest x16 12.1 us: one_block(): value_block = lax.dynamic_slice_in_dim(value_piece, turn * block, block, 0)]
    reduce_sum x11 -> x0, other arithmetic: 7.67 us -> none  [the longest x8 4.34 us: attend_block(): running_sum = running_sum * shrink + jnp.sum(weights, axis=2)]
  transfers between devices with their start and end apart: 5 -> 0, of which waited for: 5 -> 0; matrix products, arithmetic and copies ran while one was open for 6% -> 0% of each run, Pallas kernels for 0% -> 0%
where the time goes in v2:
time: 126 us
  Pallas kernels  121 us (96%)
  local copies, waits for them, and re-layouts  3.17 us (3%)
  between operations  1.95 us (2%)
    pallas_call x1, Pallas kernels, local(): pl.pallas_call(kernel, out_shape=(jax.ShapeDtypeStruct((ROWS, WIDTH), bf1...  121 us
    unnamed x7, local copies, waits for them, and re-layouts  3.17 us

profile of v2, /device:TPU:1, one launch (start us, length us, event | category | flops | bytes accessed | tf_op | source)
XLA Modules:
  0.0 126.1 jit_solution(13852988394707253341)
XLA Ops:
  1.9 121.0 %shard_map.166 = (bf16[176,640]{1,0:T(8,128)(2,1)}, f32[64,176]{1,0:T(8,128)}, f32[64,176]{1,0:T(8,128)}) custom-call(bf16[176,640]{1,0:T(8,128)(2,1)} %bitcast.20, bf16[176,640]{1,0:T(8,128)(2,1)} %bitcast.21, bf16[176,640]{1,0:T(8,128)(2,1)} %bitcast.22, bf16[176,640]{1,0:T(8,128)(2,1)} %bitcast.23, f32[1,640]{1,0:T(1,128)} %qg_ref.1, f32[1,640]{1,0:T(1,128)} %kg_ref.1, ...), custom_call_target="tpu_custom_call" | custom-call | tf_op jit(solution)/shard_map/pallas_call | solution.py:625
  122.9 0.0 copy-start.1
  122.9 1.7 %copy.23 = bf16[1,1,176,640]{3,2,1,0:T(8,128)(2,1)} copy(bf16[1,1,176,640]{3,2,1,0:T(8,128)(2,1)} %bitcast.24) | data formatting | bytes 450560
  124.6 0.0 copy-done.1
  124.6 0.0 copy-start
  124.6 0.6 copy.24
  125.2 0.2 copy-done
  125.5 0.6 copy.25
Async XLA Ops:
  122.9 1.7 %copy-start.1 = (f32[64,176]{1,0:T(8,128)S(1)}, f32[64,176]{1,0:T(8,128)}, u32[]{:S(2)}) copy-start(f32[64,176]{1,0:T(8,128)} %get-tuple-element.7) | copy-start | bytes 135172
  124.6 0.9 copy-start

commit v3 on v2

--- a/solution.py
+++ b/solution.py
@@ -67,9 +67,11 @@
 
 
 def kernel(
-    q_ref, k_ref, v_ref, res_ref, qg_ref, kg_ref, w_ref, gate_ref, scale_ref,
-    shift_ref, hw_ref, bias_ref, lat_ref, valid_ref, step_ref,
-    hid_ref, vel_ref, rel_ref,
+    q_hbm, k_hbm, v_ref, res_hbm, qg_hbm, kg_hbm, w_ref, gate_hbm, scale_hbm,
+    shift_hbm, hw_hbm, bias_hbm, lat_hbm, valid_ref, step_ref,
+    hid_hbm, vel_hbm, rel_hbm,
+    q_ref, k_ref, res_ref, qg_ref, kg_ref, gate_ref, scale_ref, shift_ref, hw_ref, bias_ref,
+    lat_ref, hid_ref, vel_ref, rel_ref, in_sem, out_sem,
     sq_pad, msg, msg_in, cos, sin, qr, kr, keys, values, queries, mask, logits, outs, att, w_mid, wg, total, px, px_in,
     head_w, bias_row, lat, pk, pk_in, swap, swap_in, fin,
     msg_ss, msg_rs, v_ss, v_rs, k_ss, k_rs, q_ss, q_rs, vr_ss, vr_rs, kr_ss, kr_rs, o_ss, o_rs,
@@ -124,6 +126,16 @@
     w_stays_mid = mid_z == z
     w_stays = jnp.logical_and(lax.rem(y, 2) == b, to_y == y)
 
+    loads = {}
+    for at, (name, src, dst) in enumerate((
+        ("q", q_hbm, q_ref), ("k", k_hbm, k_ref), ("scale", scale_hbm, scale_ref),
+        ("shift", shift_hbm, shift_ref), ("hw", hw_hbm, hw_ref), ("bias", bias_hbm, bias_ref),
+        ("lat", lat_hbm, lat_ref), ("kg", kg_hbm, kg_ref), ("qg", qg_hbm, qg_ref),
+        ("gate", gate_hbm, gate_ref), ("res", res_hbm, res_ref),
+    )):
+        loads[name] = pltpu.make_async_copy(src, dst, in_sem.at[at])
+        loads[name].start()
+
     barrier = pltpu.get_barrier_semaphore()
 
     def greet(device):
@@ -149,6 +161,8 @@
 
     sq_pad[ROWS:, :] = jnp.zeros((256 - ROWS, HD), jnp.float32)
     msg[...] = jnp.zeros_like(msg)
+    loads["q"].wait()
+    loads["k"].wait()
     for at, ref in enumerate((q_ref, k_ref)):
         row = squares(ref)
         msg[2 * at:2 * at + 1, :] = row[:, 0:HD]
@@ -201,6 +215,8 @@
     limit = valid_ref[0] * GRID_W
     key_at = lax.broadcasted_iota(jnp.int32, (1, TOKENS), 1)
     mask[...] = jnp.where(key_at < limit, 0.0, MASKED)
+    for name in ("scale", "shift", "hw", "bias", "lat", "kg", "qg"):
+        loads[name].wait()
     bias_row[...] = jnp.zeros_like(bias_row)
     bias_row[:, 0:64] = bias_ref[...]
     bias_col = jnp.broadcast_to(bias_row[...], (HD, HD)).T[0:64, 0:1]
@@ -514,8 +530,12 @@
     projected = project(b)
     arrived(px_in, px_rs)
     projected = projected + px_in[...].astype(jnp.float32)
+    loads["gate"].wait()
+    loads["res"].wait()
     hidden = (res_ref[...].astype(jnp.float32) + gate_ref[...] * projected).astype(jnp.bfloat16)
     hid_ref[...] = hidden
+    hid_out = pltpu.make_async_copy(hid_ref, hid_hbm, out_sem.at[0])
+    hid_out.start()
     hidden_f = hidden.astype(jnp.float32)
 
     over_features = (((1,), (1,)), ((), ()))
@@ -575,6 +595,12 @@
         vel_ref[4 * i:4 * i + 4, :] = fin[i, 0:4, 0:ROWS]
         rel_ref[4 * i:4 * i + 4, :] = fin[i, 4:8, 0:ROWS]
 
+    vel_out = pltpu.make_async_copy(vel_ref, vel_hbm, out_sem.at[1])
+    rel_out = pltpu.make_async_copy(rel_ref, rel_hbm, out_sem.at[2])
+    vel_out.start()
+    rel_out.start()
+
+    hid_out.wait()
     for copy in msg_copies + pk_copies + fin_copies + [swap_copy, px_copy]:
         copy.wait_send()
     sent_all(v_copies + k_copies + q_copies)
@@ -599,6 +625,8 @@
             return carry
 
         lax.fori_loop(0, 8, one, 0)
+    vel_out.wait()
+    rel_out.wait()
 
 
 def local(
@@ -618,7 +646,7 @@
     valid_rows,
     step_index,
 ):
-    vmem = pl.BlockSpec(memory_space=pltpu.VMEM)
+    hbm = pl.BlockSpec(memory_space=pl.ANY)
     smem = pl.BlockSpec(memory_space=pltpu.SMEM)
     dma = pltpu.SemaphoreType.DMA
     f32, bf16 = jnp.float32, jnp.bfloat16
@@ -629,9 +657,24 @@
             jax.ShapeDtypeStruct((64, ROWS), f32),
             jax.ShapeDtypeStruct((64, ROWS), f32),
         ),
-        in_specs=[vmem] * 13 + [smem] * 2,
-        out_specs=(vmem, vmem, vmem),
+        in_specs=[hbm] * 13 + [smem] * 2,
+        out_specs=(hbm, hbm, hbm),
         scratch_shapes=[
+            pltpu.VMEM((ROWS, WIDTH), bf16),
+            pltpu.VMEM((ROWS, WIDTH), bf16),
+            pltpu.VMEM((ROWS, WIDTH), bf16),
+            pltpu.VMEM((1, WIDTH), f32),
+            pltpu.VMEM((1, WIDTH), f32),
+            pltpu.VMEM((1, WIDTH), f32),
+            pltpu.VMEM((1, WIDTH), f32),
+            pltpu.VMEM((1, WIDTH), f32),
+            pltpu.VMEM((64, WIDTH), bf16),
+            pltpu.VMEM((1, 64), f32),
+            pltpu.VMEM((64, ROWS), f32),
+            pltpu.VMEM((ROWS, WIDTH), bf16),
+            pltpu.VMEM((64, ROWS), f32),
+            pltpu.VMEM((64, ROWS), f32),
+            dma((11,)), dma((3,)),
             pltpu.VMEM((256, HD), f32),
             pltpu.VMEM((8, HD), f32),
             pltpu.VMEM((7, 8, HD), f32),

time: 126 us -> 125 us (level)
  Pallas kernels: 121 us -> 119 us
    pallas_call x1, Pallas kernels: 121 us -> 119 us  [local(): pl.pallas_call(kernel, out_shape=(jax.ShapeDtypeStruct((ROWS, WIDTH), bf1...]
where the time goes in v3:
time: 125 us; the launch traced here: 124 us
  Pallas kernels  119 us (95%)
  local copies, waits for them, and re-layouts  3.17 us (3%)
  between operations  1.95 us (2%)
    pallas_call x1, Pallas kernels, local(): pl.pallas_call(kernel, out_shape=(jax.ShapeDtypeStruct((ROWS, WIDTH), bf1...  119 us
    unnamed x7, local copies, waits for them, and re-layouts  3.17 us

profile of v3, /device:TPU:1, one launch (start us, length us, event | category | flops | bytes accessed | tf_op | source)
XLA Modules:
  0.0 124.5 jit_solution(721635226003979904)
XLA Ops:
  1.9 119.4 %shard_map.166 = (bf16[176,640]{1,0:T(8,128)(2,1)}, f32[64,176]{1,0:T(8,128)}, f32[64,176]{1,0:T(8,128)}) custom-call(bf16[176,640]{1,0:T(8,128)(2,1)} %bitcast.20, bf16[176,640]{1,0:T(8,128)(2,1)} %bitcast.21, bf16[176,640]{1,0:T(8,128)(2,1)} %bitcast.22, bf16[176,640]{1,0:T(8,128)(2,1)} %bitcast.23, f32[1,640]{1,0:T(1,128)} %qg_hbm.1, f32[1,640]{1,0:T(1,128)} %kg_hbm.1, ...), custom_call_target="tpu_custom_call" | custom-call | tf_op jit(solution)/shard_map/pallas_call | solution.py:653
  121.3 0.0 copy-start.1
  121.3 1.7 %copy.23 = bf16[1,1,176,640]{3,2,1,0:T(8,128)(2,1)} copy(bf16[1,1,176,640]{3,2,1,0:T(8,128)(2,1)} %bitcast.24) | data formatting | bytes 450560
  123.0 0.0 copy-done.1
  123.0 0.0 copy-start
  123.0 0.6 copy.24
  123.6 0.2 copy-done
  123.9 0.6 copy.25
Async XLA Ops:
  121.3 1.7 %copy-start.1 = (f32[64,176]{1,0:T(8,128)S(1)}, f32[64,176]{1,0:T(8,128)}, u32[]{:S(2)}) copy-start(f32[64,176]{1,0:T(8,128)} %get-tuple-element.7) | copy-start | bytes 135172
  123.0 0.9 copy-start

commit v4 on v3

--- a/solution.py
+++ b/solution.py
@@ -27,6 +27,7 @@
 HEAD_Z = (0, 1, 3, 4, 6)
 UPPER = 96
 W_COPIES = 31
+PX_PARTS = ((0, 384), (384, 256))
 LIVE_FROM = 1280
 MESH = pl.DeviceIdType.MESH
 LOG2E = 1.4426950408889634
@@ -109,7 +110,10 @@
     holds = lax.rem(y + b, 2) == 0
     off = lax.rem(y + b, 2)
 
-    mid_z = 2 * lax.rem(lax.div(y, 2) + 4 - lax.div(z, 2), 4) + lax.rem(z, 2)
+    pair = lax.div(z, 2)
+    mid_pair = lax.rem(lax.div(y, 2) + 4 - pair, 4)
+    mid_odd = jnp.where(lax.rem(mid_pair + 4 - pair, 4) == 2, 1 - lax.rem(z, 2), lax.rem(z, 2))
+    mid_z = 2 * mid_pair + mid_odd
     to_y = 4 * b + lax.div(mid_z, 2)
     w_turns = lax.rem(y, 2) != b
     w_to = {
@@ -267,10 +271,13 @@
     base_x = jnp.where(turned, 1 - x_lo, x_lo)
     for dz in range(8):
         at_z = add_mod(z, dz, 8)
-        at = lax.rem(lax.div(at_z, 2) + y, 4)
+        at_pair = lax.div(at_z, 2)
+        at = lax.rem(at_pair + y, 4)
+        at_odd = lax.rem(at_z, 2)
+        at_odd = jnp.where(lax.rem(at_pair + 4 - lax.rem(y, 4), 4) == 2, 1 - at_odd, at_odd)
         for dx in range(2):
             at_x = 1 - base_x if dx else base_x
-            slots[dz, dx] = (at, (2 * lax.rem(at_z, 2) + at_x) * COLS)
+            slots[dz, dx] = (at, (2 * at_odd + at_x) * COLS)
 
     def w_slot(dz, dx, first=0, count=COLS):
         at, row = slots[dz % 8, dx]
@@ -313,7 +320,7 @@
         w_copy(("ux", j), upper(ring_slot(j), 0), beside)
 
     w_near = pltpu.make_async_copy(w_mid, w_slot(0, 0), wp_rs)
-    to_row = (2 * lax.rem(z, 2) + x_lo) * COLS
+    to_row = (2 * lax.rem(mid_z, 2) + x_lo) * COLS
     w_far = remote(
         w_mid, wg.at[lax.div(y, 2), pl.ds(pl.multiple_of(to_row, 16), COLS), :], wp_ss, wp_rs,
         w_to,
@@ -443,7 +450,7 @@
             pl.when(stays)(pltpu.make_async_copy(outs.at[at_z], att_place, o_rs.at[b, head]).start)
             pl.when(jnp.logical_not(stays))(o_far(at_z).start)
 
-        for turn, event in ((0, 'start'), (2, 'lower'), (5, 1)):
+        for turn, event in ((0, 'start'), (2, 'lower'), (6, 1)):
             pl.when(j == turn)(lambda: w_event(event))
         return carry
 
@@ -502,17 +509,15 @@
                 opposite = ag_block(way, 4, b if which else 1 - b, h)
                 arrived(opposite, ag_rs.at[way, 1, LOCAL_HEADS * which + h])
 
-    def project(tb):
-        def one_group(g, carry):
-            part = lax.dot_general(
-                att[g, tb], wg[g], (((1,), (1,)), ((), ())), preferred_element_type=jnp.float32
+    def project(tb, first, count):
+        parts = [
+            lax.dot_general(
+                att[g, tb], wg[g, first:first + count, :], (((1,), (1,)), ((), ())),
+                preferred_element_type=jnp.float32,
             )
-            total[...] += part
-            return carry
-
-        total[...] = jnp.zeros_like(total)
-        lax.fori_loop(0, 4, one_group, 0)
-        return total[...]
+            for g in range(4)
+        ]
+        return (parts[0] + parts[1]) + (parts[2] + parts[3])
 
     ag_start(0)
     w_event(2)
@@ -523,13 +528,19 @@
     ag_go_on(1)
     ag_finish(0)
     w_event('finish')
-    px[...] = project(1 - b).astype(jnp.bfloat16)
-    px_copy = remote(px, px_in, px_ss, px_rs, across)
-    px_copy.start()
+    px_copies = []
+    for at, (first, count) in enumerate(PX_PARTS):
+        cols = pl.ds(first, count)
+        px[:, first:first + count] = project(1 - b, first, count).astype(jnp.bfloat16)
+        copy = remote(px.at[:, cols], px_in.at[:, cols], px_ss.at[at], px_rs.at[at], across)
+        copy.start()
+        px_copies.append(copy)
     ag_finish(1)
-    projected = project(b)
-    arrived(px_in, px_rs)
-    projected = projected + px_in[...].astype(jnp.float32)
+    for first, count in PX_PARTS:
+        total[:, first:first + count] = project(b, first, count)
+    for at, (first, count) in enumerate(PX_PARTS):
+        arrived(px_in.at[:, pl.ds(first, count)], px_rs.at[at])
+    projected = total[...] + px_in[...].astype(jnp.float32)
     loads["gate"].wait()
     loads["res"].wait()
     hidden = (res_ref[...].astype(jnp.float32) + gate_ref[...] * projected).astype(jnp.bfloat16)
@@ -601,7 +612,7 @@
     rel_out.start()
 
     hid_out.wait()
-    for copy in msg_copies + pk_copies + fin_copies + [swap_copy, px_copy]:
+    for copy in msg_copies + pk_copies + fin_copies + px_copies + [swap_copy]:
         copy.wait_send()
     sent_all(v_copies + k_copies + q_copies)
     pl.when(jnp.logical_not(w_stays_mid))(w_mid_far.wait_send)
@@ -713,7 +724,7 @@
             dma, dma,
             dma, dma,
             dma((W_COPIES,)), dma((W_COPIES,)),
-            dma, dma,
+            dma((2,)), dma((2,)),
             dma((15,)), dma((15,)),
             dma, dma,
             dma((15,)), dma((15,)),

time: 125 us -> 123 us (0.984)
    pallas_call x1, Pallas kernels: 119 us -> 118 us  [local(): pl.pallas_call(kernel, out_shape=(jax.ShapeDtypeStruct((ROWS, WIDTH), bf1...]
where the time goes in v4:
time: 123 us
  Pallas kernels  118 us (96%)
  local copies, waits for them, and re-layouts  3.17 us (3%)
  between operations  1.95 us (2%)
    pallas_call x1, Pallas kernels, local(): pl.pallas_call(kernel, out_shape=(jax.ShapeDtypeStruct((ROWS, WIDTH), bf1...  118 us
    unnamed x7, local copies, waits for them, and re-layouts  3.17 us

profile of v4, /device:TPU:1, one launch (start us, length us, event | category | flops | bytes accessed | tf_op | source)
XLA Modules:
  0.0 122.9 jit_solution(460337464615204465)
XLA Ops:
  1.9 117.8 %shard_map.166 = (bf16[176,640]{1,0:T(8,128)(2,1)}, f32[64,176]{1,0:T(8,128)}, f32[64,176]{1,0:T(8,128)}) custom-call(bf16[176,640]{1,0:T(8,128)(2,1)} %bitcast.20, bf16[176,640]{1,0:T(8,128)(2,1)} %bitcast.21, bf16[176,640]{1,0:T(8,128)(2,1)} %bitcast.22, bf16[176,640]{1,0:T(8,128)(2,1)} %bitcast.23, f32[1,640]{1,0:T(1,128)} %qg_hbm.1, f32[1,640]{1,0:T(1,128)} %kg_hbm.1, ...), custom_call_target="tpu_custom_call" | custom-call | tf_op jit(solution)/shard_map/pallas_call | solution.py:664
  119.8 0.0 copy-start.1
  119.8 1.7 %copy.23 = bf16[1,1,176,640]{3,2,1,0:T(8,128)(2,1)} copy(bf16[1,1,176,640]{3,2,1,0:T(8,128)(2,1)} %bitcast.24) | data formatting | bytes 450560
  121.4 0.0 copy-done.1
  121.4 0.0 copy-start
  121.4 0.6 copy.24
  122.1 0.2 copy-done
  122.3 0.6 copy.25
Async XLA Ops:
  119.8 1.7 %copy-start.1 = (f32[64,176]{1,0:T(8,128)S(1)}, f32[64,176]{1,0:T(8,128)}, u32[]{:S(2)}) copy-start(f32[64,176]{1,0:T(8,128)} %get-tuple-element.7) | copy-start | bytes 135172
  121.4 0.9 copy-start
